TPU v7x, 256 devices: a whole 4x4x8 slice. The times are simulated.
256 devices in a mesh: expert: 32 (over x, z), half: 2 (over core), dp: 4 (over y).
Axes of the slice: x: 4, y: 4, z: 8, core: 2. Of those that a mesh axis runs over, the one named last changes fastest.
Arguments:
- tokens_in: bfloat16 [128, 2, 12, 3584], P(('expert', 'dp')), may hold values from -6 to 6
- cotangent: bfloat16 [128, 2, 12, 3584], P(('expert', 'dp')), may hold values from -1.5 to 1.5
- expert_ids: int32 [128, 2, 12, 8], P(('expert', 'dp')), may hold values from 0 to 31, all different within a row; in each aligned block of 12 rows (0 to 11, 12 to 23, ..., all dimensions but the last counted through in order) at most 6 rows name the same one
- gate_probs: bfloat16 [128, 2, 12, 8], P(('expert', 'dp')), may hold values from 0.049804688 to 0.5
- gate_weight: bfloat16 [32, 3584, 1024], P('expert', 'dp', 'half'), may hold values from -0.09375 to 0.09375
- up_weight: bfloat16 [32, 3584, 1024], P('expert', 'dp', 'half'), may hold values from -0.09375 to 0.09375
- down_weight: bfloat16 [32, 3584, 1024], P('expert', 'dp', 'half'), may hold values from -0.1875 to 0.1875
Outputs:
- token_grad: bfloat16 [128, 2, 12, 3584], P(('expert', 'dp'), 'half')
- route_grad: bfloat16 [128, 2, 12, 8], P(('expert', 'dp'), 'half')
- gate_weight_grad: bfloat16 [32, 3584, 1024], P('expert', 'dp', 'half')
- up_weight_grad: bfloat16 [32, 3584, 1024], P('expert', 'dp', 'half')
- down_weight_grad: bfloat16 [32, 3584, 1024], P('expert', 'dp', 'half')
Inputs may be any that keep to these rules, and one draw needn't show every extreme that they name: `expert_ids`: each row names 8 different experts. Among the 12 tokens of one owner block (the aligned blocks of the last two leading dimensions), no expert is named by more than 6 tokens, and in every draw some expert is named by exactly 6 tokens of some block.
All inputs are finite; a program needn't handle non-finite values.
Results may differ from a plain program's by a relative error of at most 0.017.
Values may be sent and summed in bfloat16 or wider, within the bound.
A program may use at most 192 MiB of HBM per device.

v0:
```python
import jax
import jax.numpy as jnp
from jax import lax
from jax.sharding import PartitionSpec as P

MOST = 6


def route_slots(route_ids, route_gates, expert_count):
    experts_here = jnp.arange(expert_count, dtype=jnp.int32)
    matched = route_ids[..., None, :, :] == experts_here[:, None, None]
    chosen = jnp.any(matched, axis=-1)
    slot_rank = jnp.cumsum(chosen.astype(jnp.int32), axis=-1) - 1
    slot_ids = jnp.arange(MOST, dtype=jnp.int32)
    slot_pick = jnp.logical_and(chosen[..., None, :], slot_rank[..., None, :] == slot_ids[:, None])
    route_gate = jnp.sum(
        jnp.where(matched, route_gates.astype(jnp.float32)[..., None, :, :], 0.0), axis=-1
    )
    slot_gate = jnp.sum(jnp.where(slot_pick, route_gate[..., None, :], 0.0), axis=-1)
    return (slot_pick, matched, slot_gate)


def silu_parts(pre_act):
    sigma = jax.nn.sigmoid(pre_act)
    return (pre_act * sigma, sigma * (1.0 + pre_act * (1.0 - sigma)))


def expert_rows(flat_x, flat_dy, gate_col, w_gate, w_up, w_down):
    gate_act = jnp.dot(flat_x, w_gate, preferred_element_type=jnp.float32)
    up_act = jnp.dot(flat_x, w_up, preferred_element_type=jnp.float32)
    back_act = jnp.dot(flat_dy, w_down, preferred_element_type=jnp.float32)
    active, silu_slope = silu_parts(gate_act)
    hidden = (active * up_act).astype(jnp.bfloat16)
    grad_gate = (gate_col * back_act * up_act * silu_slope).astype(jnp.bfloat16)
    grad_up = (gate_col * back_act * active).astype(jnp.bfloat16)
    scaled = (gate_col * flat_dy.astype(jnp.float32)).astype(jnp.bfloat16)
    by_column = (((1,), (1,)), ((), ()))
    by_row = (((0,), (0,)), ((), ()))
    row_part = lax.dot_general(
        grad_gate, w_gate, by_column, preferred_element_type=jnp.float32
    ) + lax.dot_general(grad_up, w_up, by_column, preferred_element_type=jnp.float32)
    route_part = jnp.sum(back_act * hidden.astype(jnp.float32), axis=1)
    term = jnp.concatenate(
        [
            lax.dot_general(flat_x, grad_gate, by_row, preferred_element_type=jnp.float32),
            lax.dot_general(flat_x, grad_up, by_row, preferred_element_type=jnp.float32),
            lax.dot_general(scaled, hidden, by_row, preferred_element_type=jnp.float32),
        ],
        axis=1,
    )
    return (row_part, route_part, term)


def collect_rows(back_rows, back_route, pick_bf, matched, half_index, all_experts, model_width):
    back_rows = back_rows.reshape(all_experts, MOST, model_width)
    back_route = back_route.reshape(all_experts, MOST)
    own_pick = lax.dynamic_index_in_dim(pick_bf, half_index, 0, keepdims=False)
    own_match = lax.dynamic_index_in_dim(matched, half_index, 0, keepdims=False)
    token_sum = jnp.einsum("est,esd->td", own_pick, back_rows, preferred_element_type=jnp.float32)
    per_token = jnp.einsum(
        "est,es->et", own_pick.astype(jnp.float32), back_route.astype(jnp.float32)
    )
    route_sum = jnp.sum(jnp.where(own_match, per_token[:, :, None], 0.0), axis=0)
    return (token_sum, route_sum)


def on_device(tokens_in, cotangent, expert_ids, gate_probs, gate_weight, up_weight, down_weight):
    n_expert = lax.axis_size("expert")
    per_device = gate_weight.shape[0]
    all_experts = n_expert * per_device
    half_index = lax.axis_index("half")
    model_width = tokens_in.shape[3]
    hidden_width = gate_weight.shape[2]
    w_gate, w_up, w_down = (
        lax.all_gather(gate_weight, "dp", axis=1, tiled=True),
        lax.all_gather(up_weight, "dp", axis=1, tiled=True),
        lax.all_gather(down_weight, "dp", axis=1, tiled=True),
    )
    slot_pick, matched, slot_gate = route_slots(expert_ids[0], gate_probs[0], all_experts)
    pick_bf = slot_pick.astype(jnp.bfloat16)
    send_x = jnp.einsum(
        "hest,htd->ehsd", pick_bf, tokens_in[0], preferred_element_type=jnp.float32
    ).astype(jnp.bfloat16)
    send_dy = jnp.einsum(
        "hest,htd->ehsd", pick_bf, cotangent[0], preferred_element_type=jnp.float32
    ).astype(jnp.bfloat16)
    send_gate = jnp.transpose(slot_gate, (1, 0, 2)).astype(jnp.bfloat16)
    shaped = (n_expert, per_device, 2, MOST)
    recv_x, recv_dy, recv_gate = (
        lax.all_to_all(
            send_x.reshape(shaped + (model_width,)),
            "expert",
            split_axis=0,
            concat_axis=0,
            tiled=True,
        ),
        lax.all_to_all(
            send_dy.reshape(shaped + (model_width,)),
            "expert",
            split_axis=0,
            concat_axis=0,
            tiled=True,
        ),
        lax.all_to_all(
            send_gate.reshape(shaped), "expert", split_axis=0, concat_axis=0, tiled=True
        ),
    )
    flat_x = recv_x[:, 0].reshape(-1, model_width)
    flat_dy = recv_dy[:, 0].reshape(-1, model_width)
    flat_gate = recv_gate[:, 0].reshape(-1)
    row_part, route_part, term = expert_rows(
        flat_x, flat_dy, flat_gate.astype(jnp.float32)[:, None], w_gate[0], w_up[0], w_down[0]
    )
    row_parts = [row_part.reshape(n_expert, 2, MOST, model_width)]
    route_parts = [route_part.reshape(n_expert, 2, MOST)]
    term_parts = [term]
    row_total = jnp.stack(row_parts, axis=1)
    route_total = jnp.stack(route_parts, axis=1)
    term_all = jnp.stack(term_parts, axis=1)
    summed_rows, summed_route = (
        lax.psum(row_total.astype(jnp.bfloat16), "half").astype(jnp.float32),
        lax.psum(route_total.astype(jnp.bfloat16), "half").astype(jnp.float32),
    )
    own_rows = lax.dynamic_index_in_dim(summed_rows, half_index, 2, keepdims=False)
    own_route = lax.dynamic_index_in_dim(summed_route, half_index, 2, keepdims=False)
    row_grad = own_rows.astype(jnp.bfloat16)
    row_route = own_route.astype(jnp.bfloat16)
    back_rows, back_route = (
        lax.all_to_all(row_grad, "expert", split_axis=0, concat_axis=0, tiled=True),
        lax.all_to_all(row_route, "expert", split_axis=0, concat_axis=0, tiled=True),
    )
    token_sum, route_sum = collect_rows(
        back_rows, back_route, pick_bf, matched, half_index, all_experts, model_width
    )
    token_grad = token_sum.astype(jnp.bfloat16)[None, None]
    route_grad = route_sum.astype(jnp.bfloat16)[None, None]
    term_flat = term_all.reshape(model_width, -1)
    rounded = lax.optimization_barrier(term_flat.astype(jnp.bfloat16)).astype(jnp.float32)
    shard_rows = model_width // lax.axis_size("dp")
    summed = lax.psum_scatter(rounded.astype(jnp.bfloat16), "dp", scatter_dimension=0, tiled=True)
    summed = summed.reshape(shard_rows, per_device, 3, hidden_width)
    gate_weight_grad = jnp.transpose(summed[:, :, 0], (1, 0, 2))
    up_weight_grad = jnp.transpose(summed[:, :, 1], (1, 0, 2))
    down_weight_grad = jnp.transpose(summed[:, :, 2], (1, 0, 2))
    return (token_grad, route_grad, gate_weight_grad, up_weight_grad, down_weight_grad)


def solution(mesh):
    return jax.shard_map(
        on_device,
        mesh=mesh,
        in_specs=(
            P(("expert", "dp"), None, None, None),
            P(("expert", "dp"), None, None, None),
            P(("expert", "dp"), None, None, None),
            P(("expert", "dp"), None, None, None),
            P("expert", "dp", "half"),
            P("expert", "dp", "half"),
            P("expert", "dp", "half"),
        ),
        out_specs=(
            P(("expert", "dp"), "half", None, None),
            P(("expert", "dp"), "half", None, None),
            P("expert", "dp", "half"),
            P("expert", "dp", "half"),
            P("expert", "dp", "half"),
        ),
        check_vma=False,
    )
```

profile of v0, /device:TPU:6, one launch (start us, length us, event | category | flops | bytes accessed | tf_op | source)
XLA Modules:
  0.0 362.3 jit_solution(6658443864269046373)
XLA Ops:
  7.2 0.7 all-gather.8.cloned.1.call-update
  7.9 0.7 bitcast_convert_fusion
  8.7 0.8 copy.95
  9.8 0.7 copy.97
  10.6 11.6 %all-to-all-start = ((bf16[32,1,2,6]{3,2,1,0:T(2,128)(2,1)}), bf16[32,1,2,6]{3,2,1,0:T(2,128)(2,1)S(1)}, u32[]{:S(2)}, u32[]{:S(2)}) async-start(bf16[32,1,2,6]{3,2,1,0:T(2,128)(2,1)} %copy.97), calls=%async_computation | async-start | bytes 32768 | tf_op jit(solution)/shard_map/all_to_all | solution.py:104
  22.2 0.9 fusion.1
  23.1 4.4 %copy.99 = bf16[32,1,2,6,3584]{4,2,3,1,0:T(2,128)(2,1)} copy(bf16[32,1,2,6,3584]{4,0,3,2,1:T(8,128)(2,1)S(1)} %fusion.1) | data formatting | bytes 5505024 | tf_op jit(solution)/shard_map/reshape | solution.py:98
  27.5 2.5 all-to-all-done
  30.0 7.5 %all-to-all-start.1 = ((bf16[32,1,2,6,3584]{4,2,3,1,0:T(2,128)(2,1)}), bf16[32,1,2,6,3584]{4,2,3,1,0:T(2,128)(2,1)S(1)}, u32[]{:S(2)}, u32[]{:S(2)}) async-start(bf16[32,1,2,6,3584]{4,2,3,1,0:T(2,128)(2,1)} %copy.99), calls=%async_computation.1 | async-start | bytes 5505024 | tf_op jit(solution)/shard_map/all_to_all | solution.py:97
  37.5 0.7 all-gather.6.cloned.1.call-update
  38.2 0.9 fusion.2
  39.2 4.4 %copy.102 = bf16[32,1,2,6,3584]{4,2,3,1,0:T(2,128)(2,1)} copy(bf16[32,1,2,6,3584]{4,0,3,2,1:T(8,128)(2,1)S(1)} %fusion.2) | data formatting | bytes 5505024 | tf_op jit(solution)/shard_map/reshape | solution.py:91
  43.5 57.5 %all-to-all-done.1 = bf16[32,1,2,6,3584]{4,2,3,1,0:T(2,128)(2,1)S(1)} async-done(((bf16[32,1,2,6,3584]{4,2,3,1,0:T(2,128)(2,1)}), bf16[32,1,2,6,3584]{4,2,3,1,0:T(2,128)(2,1)S(1)}, u32[]{:S(2)}, u32[]{:S(2)}) %all-to-all-start.1) | async-done | bytes 2752544 | tf_op jit(solution)/shard_map/all_to_all | solution.py:97
  101.0 6.8 %all-to-all-start.2 = ((bf16[32,1,2,6,3584]{4,2,3,1,0:T(2,128)(2,1)}), bf16[32,1,2,6,3584]{4,2,3,1,0:T(2,128)(2,1)}, u32[]{:S(2)}, u32[]{:S(2)}) async-start(bf16[32,1,2,6,3584]{4,2,3,1,0:T(2,128)(2,1)} %copy.102), calls=%async_computation.2 | async-start | bytes 5505024 | tf_op jit(solution)/shard_map/all_to_all | solution.py:90
  107.9 0.7 all-gather.4.cloned.1.call-update
  109.0 2.5 copy.100
  111.4 4.0 %reshape_squeeze.7 = bf16[384,3584]{1,0:T(8,128)(2,1)S(1)} reshape(bf16[32,1,2,6,3584]{4,3,2,0,1:T(8,128)(2,1)} %copy.100) | data formatting | bytes 5505024 | tf_op jit(solution)/shard_map/reshape;squeeze | solution.py:109
  115.4 56.0 %all-to-all-done.2 = bf16[32,1,2,6,3584]{4,2,3,1,0:T(2,128)(2,1)} async-done(((bf16[32,1,2,6,3584]{4,2,3,1,0:T(2,128)(2,1)}), bf16[32,1,2,6,3584]{4,2,3,1,0:T(2,128)(2,1)}, u32[]{:S(2)}, u32[]{:S(2)}) %all-to-all-start.2) | async-done | bytes 2752544 | tf_op jit(solution)/shard_map/all_to_all | solution.py:90
  171.5 4.3 %copy.103 = bf16[32,1,2,6,3584]{4,3,2,0,1:T(8,128)(2,1)} copy(bf16[32,1,2,6,3584]{4,2,3,1,0:T(2,128)(2,1)} %all-to-all-done.2) | data formatting | bytes 5505024 | tf_op jit(solution)/shard_map/all_to_all | solution.py:90
  175.7 5.5 %reshape_squeeze.8 = bf16[384,3584]{1,0:T(8,128)(2,1)} reshape(bf16[32,1,2,6,3584]{4,3,2,0,1:T(8,128)(2,1)} %copy.103) | data formatting | bytes 5505024 | tf_op jit(solution)/shard_map/reshape;squeeze | solution.py:108
  181.2 5.3 %fusion.7 = f32[384,512]{1,0:T(8,128)} fusion(bf16[384,3584]{1,0:T(8,128)(2,1)} %reshape_squeeze.8, bf16[1,3584,512]{2,1,0:T(8,128)(2,1)} %all-gather.8.cloned.1.call-done), kind=kOutput, calls=%fused_computation.16 | convolution fusion | flops 1409286144 | bytes 7208960 | tf_op jit(solution)/shard_map/dot_general | solution.py:29
  186.5 5.3 %fusion.10 = f32[384,512]{1,0:T(8,128)} fusion(bf16[384,3584]{1,0:T(8,128)(2,1)} %reshape_squeeze.8, bf16[1,3584,512]{2,1,0:T(8,128)(2,1)} %all-gather.6.cloned.1.call-done), kind=kOutput, calls=%fused_computation.19 | convolution fusion | flops 1409286144 | bytes 7208960 | tf_op jit(solution)/shard_map/dot_general | solution.py:30
  191.9 5.3 %multiply_reduce_fusion = (bf16[384]{0:T(512)(128)(2,1)S(1)}, bf16[384,512]{1,0:T(8,128)(2,1)}, bf16[384,512]{1,0:T(8,128)(2,1)S(1)}, bf16[384,512]{1,0:T(8,128)(2,1)S(1)}) fusion(f32[384,512]{1,0:T(8,128)} %fusion.10, f32[384,512]{1,0:T(8,128)} %fusion.7, f32[384]{0:T(512)S(1)} %reshape.122, bf16[384,3584]{1,0:T(8,128)(2,1)S(1)} %reshape_squeeze.7, ...), kind=kOutput, calls=%fused_computation.28 | convolution fusion | flops 1413021312 | bytes 9177344 | tf_op jit(solution)/shard_map/dot_general | solution.py:31
  197.2 1.6 fusion.5
  198.8 0.5 copy-done.3
  199.3 1.6 fusion
  201.0 2.7 convert_element_type.161
  204.0 1.5 copy-done.7
  205.5 3.1 convolution_convert_fusion.1
  208.6 2.1 convolution_convert_fusion.2
  210.7 2.2 convolution_convert_fusion
  212.9 14.9 %pad_maximum_fusion = bf16[3584,1536]{0,1:T(8,128)(2,1)} fusion(bf16[3584,512]{0,1:T(8,128)(2,1)S(1)} %convolution_convert_fusion, bf16[3584,512]{0,1:T(8,128)(2,1)S(1)} %convolution_convert_fusion.1, bf16[3584,512]{0,1:T(8,128)(2,1)S(1)} %convolution_convert_fusion.2), kind=kLoop, calls=%fused_computation | loop fusion | flops 33030144 | bytes 22020096 | tf_op jit(solution)/shard_map/concatenate | solution.py:43
  227.8 15.0 %copy.123 = bf16[3584,1536]{1,0:T(8,128)(2,1)} copy(bf16[3584,1536]{0,1:T(8,128)(2,1)} %pad_maximum_fusion) | data formatting | bytes 22020096
  243.1 2.5 psum.15
  245.5 0.7 copy.107
  246.3 6.2 %all-to-all-start.4 = ((bf16[32,1,6]{2,1,0:T(2,128)(2,1)}), bf16[32,1,6]{2,1,0:T(2,128)(2,1)S(1)}, u32[]{:S(2)}, u32[]{:S(2)}) async-start(bf16[32,1,6]{2,1,0:T(2,128)(2,1)} %copy.107), calls=%async_computation.4 | async-start | bytes 32768 | tf_op jit(solution)/shard_map/all_to_all | solution.py:130
  252.5 3.1 fusion.15
  255.6 4.7 %all-to-all-done.4 = bf16[32,1,6]{2,1,0:T(2,128)(2,1)S(1)} async-done(((bf16[32,1,6]{2,1,0:T(2,128)(2,1)}), bf16[32,1,6]{2,1,0:T(2,128)(2,1)S(1)}, u32[]{:S(2)}, u32[]{:S(2)}) %all-to-all-start.4) | async-done | bytes 416 | tf_op jit(solution)/shard_map/all_to_all | solution.py:130
  260.3 5.9 %all-to-all-start.3 = ((bf16[32,1,6,3584]{3,2,1,0:T(8,128)(2,1)}), bf16[32,1,6,3584]{3,2,1,0:T(8,128)(2,1)S(1)}, u32[]{:S(2)}, u32[]{:S(2)}) async-start(bf16[32,1,6,3584]{3,2,1,0:T(8,128)(2,1)} %fusion.15), calls=%async_computation.3 | async-start | bytes 3670016 | tf_op jit(solution)/shard_map/all_to_all | solution.py:129
  266.4 0.7 copy.109
  267.1 41.0 %all-to-all-done.3 = bf16[32,1,6,3584]{3,2,1,0:T(8,128)(2,1)S(1)} async-done(((bf16[32,1,6,3584]{3,2,1,0:T(8,128)(2,1)}), bf16[32,1,6,3584]{3,2,1,0:T(8,128)(2,1)S(1)}, u32[]{:S(2)}, u32[]{:S(2)}) %all-to-all-start.3) | async-done | bytes 1376288 | tf_op jit(solution)/shard_map/all_to_all | solution.py:129
  308.1 1.1 fusion.4
  309.2 35.8 %reduce-scatter.4.cloned.1.call-done = bf16[896,1536]{1,0:T(8,128)(2,1)} async-done(((bf16[3584,1536]{1,0:T(8,128)(2,1)}), bf16[896,1536]{1,0:T(8,128)(2,1)}) %reduce-scatter.4.cloned.1.call-update) | async-done | bytes 2752528
  345.1 3.3 copy.124
  348.4 1.6 fusion.29
  350.0 2.3 copy.127
  352.3 2.2 copy.126
  354.5 1.3 copy.125
  (47 shorter events, 1.8 us)
Async XLA Ops:
  7.2 15.0 %copy-start = (bf16[1,2,12,3584]{3,1,2,0:T(2,128)(2,1)S(1)}, bf16[1,2,12,3584]{3,1,2,0:T(2,128)(2,1)}, u32[]{:S(2)}) copy-start(bf16[1,2,12,3584]{3,1,2,0:T(2,128)(2,1)} %param.8) | copy-start | bytes 516100
  7.2 174.0 %all-gather.8.cloned.1.call-start = ((), (), s32[]{:S(2)}) async-start(), calls=%async_computation.8 | async-start | bytes 4587520 | tf_op jit(solution)/shard_map/all_gather | solution.py:75
  10.6 19.4 %all-to-all-start = ((bf16[32,1,2,6]{3,2,1,0:T(2,128)(2,1)}), bf16[32,1,2,6]{3,2,1,0:T(2,128)(2,1)S(1)}, u32[]{:S(2)}, u32[]{:S(2)}) async-start(bf16[32,1,2,6]{3,2,1,0:T(2,128)(2,1)} %copy.97), calls=%async_computation | async-start | bytes 32768 | tf_op jit(solution)/shard_map/all_to_all | solution.py:104
  27.5 10.7 %copy-start.9 = (bf16[1,2,12,3584]{3,1,2,0:T(2,128)(2,1)S(1)}, bf16[1,2,12,3584]{3,1,2,0:T(2,128)(2,1)}, u32[]{:S(2)}) copy-start(bf16[1,2,12,3584]{3,1,2,0:T(2,128)(2,1)} %param.7) | copy-start | bytes 516100
  30.0 71.0 %all-to-all-start.1 = ((bf16[32,1,2,6,3584]{4,2,3,1,0:T(2,128)(2,1)}), bf16[32,1,2,6,3584]{4,2,3,1,0:T(2,128)(2,1)S(1)}, u32[]{:S(2)}, u32[]{:S(2)}) async-start(bf16[32,1,2,6,3584]{4,2,3,1,0:T(2,128)(2,1)} %copy.99), calls=%async_computation.1 | async-start | bytes 5505024 | tf_op jit(solution)/shard_map/all_to_all | solution.py:97
  37.5 149.1 %all-gather.6.cloned.1.call-start = ((), (), s32[]{:S(2)}) async-start(), calls=%async_computation.7 | async-start | bytes 4587520 | tf_op jit(solution)/shard_map/all_gather | solution.py:76
  101.0 70.4 %all-to-all-start.2 = ((bf16[32,1,2,6,3584]{4,2,3,1,0:T(2,128)(2,1)}), bf16[32,1,2,6,3584]{4,2,3,1,0:T(2,128)(2,1)}, u32[]{:S(2)}, u32[]{:S(2)}) async-start(bf16[32,1,2,6,3584]{4,2,3,1,0:T(2,128)(2,1)} %copy.102), calls=%async_computation.2 | async-start | bytes 5505024 | tf_op jit(solution)/shard_map/all_to_all | solution.py:90
  107.9 84.0 %all-gather.4.cloned.1.call-start = ((), (), s32[]{:S(2)}) async-start(), calls=%async_computation.6 | async-start | bytes 4587520 | tf_op jit(solution)/shard_map/all_gather | solution.py:77
  108.6 143.9 %all-reduce.2.cloned.1.call-start = ((), (), s32[]{:S(2)}) async-start(), calls=%async_computation.9 | async-start | bytes 7340032 | tf_op jit(solution)/shard_map/psum | solution.py:121
  115.4 76.5 %copy-start.5 = (bf16[384,3584]{1,0:T(8,128)(2,1)}, bf16[384,3584]{1,0:T(8,128)(2,1)S(1)}, u32[]{:S(2)}) copy-start(bf16[384,3584]{1,0:T(8,128)(2,1)S(1)} %reshape_squeeze.7) | copy-start | bytes 8257540
  191.9 5.3 %copy-start.2 = (bf16[1,3584,512]{2,1,0:T(8,128)(2,1)S(1)}, bf16[1,3584,512]{2,1,0:T(8,128)(2,1)}, u32[]{:S(2)}) copy-start(bf16[1,3584,512]{2,1,0:T(8,128)(2,1)} %all-gather.8.cloned.1.call-done) | copy-start | bytes 11010052
  197.1 1.6 copy-start.8
  197.2 2.2 copy-start.3
  203.7 1.8 copy-start.7
  203.7 141.3 %reduce-scatter.4.cloned.1.call-start = ((), (), s32[]{:S(2)}) async-start(), calls=%async_computation.10 | async-start | bytes 13762560
  208.6 2.1 copy-start.6
  208.6 2.1 copy-start.10
  246.3 14.0 %all-to-all-start.4 = ((bf16[32,1,6]{2,1,0:T(2,128)(2,1)}), bf16[32,1,6]{2,1,0:T(2,128)(2,1)S(1)}, u32[]{:S(2)}, u32[]{:S(2)}) async-start(bf16[32,1,6]{2,1,0:T(2,128)(2,1)} %copy.107), calls=%async_computation.4 | async-start | bytes 32768 | tf_op jit(solution)/shard_map/all_to_all | solution.py:130
  260.3 47.8 %all-to-all-start.3 = ((bf16[32,1,6,3584]{3,2,1,0:T(8,128)(2,1)}), bf16[32,1,6,3584]{3,2,1,0:T(8,128)(2,1)S(1)}, u32[]{:S(2)}, u32[]{:S(2)}) async-start(bf16[32,1,6,3584]{3,2,1,0:T(8,128)(2,1)} %fusion.15), calls=%async_computation.3 | async-start | bytes 3670016 | tf_op jit(solution)/shard_map/all_to_all | solution.py:129
  348.3 7.4 %copy-start.1 = (bf16[1,2,12,3584]{3,1,2,0:T(2,128)(2,1)S(1)}, bf16[1,2,12,3584]{3,1,2,0:T(2,128)(2,1)}, u32[]{:S(2)}) copy-start(bf16[1,2,12,3584]{3,1,2,0:T(2,128)(2,1)} %param.8) | copy-start | bytes 516100
  350.0 4.5 %copy-start.4 = (bf16[896,1,1,512]{0,3,2,1:T(8,128)(2,1)S(1)}, bf16[896,1,1,512]{0,3,2,1:T(8,128)(2,1)}, u32[]{:S(2)}) copy-start(bf16[896,1,1,512]{0,3,2,1:T(8,128)(2,1)} %get-tuple-element.9) | copy-start | bytes 2752516
Sparse Core Ops, SparseCore 0:
  9.8 49.3 all-gather.7
  61.1 46.7 all-gather.5
  110.5 47.5 all-gather.3
  203.8 32.7 all-reduce.1
  242.9 102.0 reduce-scatter.3
where the time goes:
time: 365 us; the launch traced here: 362 us
  waiting for transfers between devices  200 us (55%)
  local copies, waits for them, and re-layouts  58.9 us (16%)
  starting transfers between devices  38.5 us (11%)
  matrix products  29.6 us (8%)
  other arithmetic  19.2 us (5%)
  between operations  14 us (4%)
    all_to_all x1, waiting for transfers between devices, on_device(): lax.all_to_all(send_dy.reshape(shaped + (model_width,)), 'expert', split_...  57.5 us
    all_to_all x1, waiting for transfers between devices, on_device(): lax.all_to_all(send_x.reshape(shaped + (model_width,)), 'expert', split_a...  56 us
    all_to_all x1, waiting for transfers between devices, on_device(): lax.all_to_all(row_grad, 'expert', split_axis=0, concat_axis=0, tiled=True)  41 us
    unnamed x6, waiting for transfers between devices  37.9 us
    unnamed x27, local copies, waits for them, and re-layouts  26.1 us
    concatenate x1, other arithmetic, expert_rows(): jnp.concatenate([lax.dot_general(flat_x, grad_gate, by_row, preferred_ele...  14.9 us
    all_to_all x1, starting transfers between devices, on_device(): lax.all_to_all(send_gate.reshape(shaped), 'expert', split_axis=0, concat_...  11.6 us
    all_to_all x1, starting transfers between devices, on_device(): lax.all_to_all(send_dy.reshape(shaped + (model_width,)), 'expert', split_...  7.45 us
  transfers between devices with their start and end apart: 10, of which 6 were waited for; matrix products, arithmetic and copies ran while one was open for 23% of the time, Pallas kernels for 0%

commit v1 on v0

v1 whole, which is shorter than its diff:
```python
import functools

import jax
import jax.numpy as jnp
import numpy as np
from jax import lax
from jax.experimental import pallas as pl
from jax.experimental.pallas import tpu as pltpu
from jax.sharding import PartitionSpec as P

MESH = pl.DeviceIdType.MESH
BF16 = jnp.bfloat16
F32 = jnp.float32

MOST = 6
TOK = 12
PAD = 16
NX, NY, NZ = 4, 4, 8
RING = NX * NZ
LAST = RING // 2
SPAN = 4
CHUNKS = RING // SPAN
UNIT_TOK = NY * TOK
UNIT = NY * MOST
TOKENS = 2 * SPAN * UNIT_TOK
SLOTS = 2 * SPAN * UNIT
PART = SLOTS // NY
LANES = 128


def rem(a, b):
    return lax.rem(a, jnp.int32(b))


def div(a, b):
    return lax.div(a, jnp.int32(b))


def ring_position(expert, half):
    x, z = div(expert, NZ), rem(expert, NZ)
    first = 4 * z + rem(x + z, 4)
    turn = rem(z + 5 * x, NZ)
    second = 4 * x + 16 * div(turn, 4) + rem(turn, 4)
    return first + half * (second - first)


def ring_expert(position, half):
    group, inner = div(position, 4), rem(position, 4)
    first = rem(inner + 3 * group, NX) * NZ + group
    second = rem(group, NX) * NZ + rem(3 * group + inner, NZ)
    return first + half * (second - first)


def matmul(a, b, a_dim=1, b_dim=0):
    return lax.dot_general(a, b, (((a_dim,), (b_dim,)), ((), ())), preferred_element_type=F32)


def kernel(
    width,
    hidden,
    stage,
    w_gate,
    w_up,
    w_down,
    ids,
    before_chunk,
    slot_base,
    squeeze,
    before_own,
    spread,
    gather,
    slot_of,
    same_part,
    token_out,
    route_out,
    gate_out,
    up_out,
    down_out,
    own,
    unit_x,
    unit_d,
    slot_x,
    slot_s,
    gates,
    part,
    sum_one,
    sum_two,
    act,
    row_part,
    row_other,
    row_send,
    row_back,
    fin_send,
    fin_recv,
    acc,
    own_sem,
    ring_sem,
    twin_sem,
    sum_sem,
    act_sem,
    half_sem,
    back_send,
    back_recv,
    fin_sem,
):
    expert, half, dp = lax.axis_index("expert"), lax.axis_index("half"), lax.axis_index("dp")
    other = 1 - half
    position = ring_position(expert, half)
    ahead = ring_expert(rem(position + 1, RING), half)
    behind = ring_expert(rem(position + RING - 1, RING), half)
    y_next, y_last, y_far = rem(dp + 1, NY), rem(dp + 3, NY), rem(dp + 2, NY)
    three = 3 * hidden
    mid = three // 2

    def remote(src, dst, send, recv, where):
        return pltpu.make_async_remote_copy(
            src_ref=src, dst_ref=dst, send_sem=send, recv_sem=recv, device_id=where, device_id_type=MESH
        )

    barrier = pltpu.get_barrier_semaphore()

    def greet(i, carry):
        pl.semaphore_signal(
            barrier, inc=1, device_id={"expert": rem(expert + i, RING)}, device_id_type=MESH
        )
        return carry

    lax.fori_loop(1, RING, greet, 0)
    for r in range(1, NY):
        pl.semaphore_signal(barrier, inc=1, device_id={"dp": rem(dp + r, NY)}, device_id_type=MESH)
    pl.semaphore_signal(barrier, inc=1, device_id={"half": other}, device_id_type=MESH)
    pl.semaphore_wait(barrier, RING - 1 + NY - 1 + 1)

    def own_copy(r):
        return remote(
            stage.at[rem(dp + r, NY)],
            own.at[dp],
            own_sem.at[0, r],
            own_sem.at[1, r],
            {"dp": rem(dp + r, NY)},
        )

    def own_arrival(r):
        source = rem(dp + NY - r, NY)
        return remote(stage.at[source], own.at[source], own_sem.at[0, r], own_sem.at[1, r], {"dp": source})

    for r in range(1, NY):
        own_copy(r).start()
    own[dp] = stage[dp]
    acc[...] = jnp.zeros_like(acc)
    for r in range(1, NY):
        own_arrival(r).wait_recv()
    own_rows = own[...].reshape(NY * PAD, 2 * width + LANES)
    packed = matmul(squeeze[...], own_rows).astype(BF16)
    unit_x[half, 0] = packed[:, : width + LANES]
    unit_d[half, 0] = packed[:, width + LANES :]

    def ring_x(step, toward, src, dst):
        way = 0 if toward is ahead else 1
        return remote(
            unit_x.at[half, src],
            unit_x.at[half, dst],
            ring_sem.at[0, 0, way, step - 1],
            ring_sem.at[0, 1, way, step - 1],
            {"expert": toward},
        )

    def ring_d(step, toward, src, dst):
        way = 0 if toward is ahead else 1
        return remote(
            unit_d.at[half, src],
            unit_d.at[half, dst],
            ring_sem.at[1, 0, way, step - 1],
            ring_sem.at[1, 1, way, step - 1],
            {"expert": toward},
        )

    ring_x(1, ahead, 0, 2).start()
    ring_x(1, behind, 0, 1).start()
    ring_d(1, ahead, 0, 2).start()
    ring_d(1, behind, 0, 1).start()

    def ring_step(step):
        fore, aft = 2 * step - 1, 2 * step
        more, inner = step + 1 < LAST, step < LAST
        ring_x(step, behind, fore, fore).wait_recv()

        @pl.when(inner)
        def _():
            ring_x(step + 1, behind, fore, fore + 2).start()
            ring_d(step, behind, fore, fore).wait_recv()
            ring_x(step, ahead, aft, aft).wait_recv()

        @pl.when(more)
        def _():
            ring_d(step + 1, behind, fore, fore + 2).start()
            ring_x(step + 1, ahead, aft, aft + 2).start()

        @pl.when(inner)
        def _():
            ring_d(step, ahead, aft, aft).wait_recv()

        @pl.when(more)
        def _():
            ring_d(step + 1, ahead, aft, aft + 2).start()

        @pl.when(step == LAST - 1)
        def _():
            ring_d(step + 1, ahead, aft, fore + 2).start()

        @pl.when(step == LAST)
        def _():
            ring_d(step, ahead, fore, fore).wait_recv()

    def twin_x(c, block):
        span = pl.ds(c * SPAN, SPAN)
        return remote(
            unit_x.at[block, span],
            unit_x.at[block, span],
            twin_sem.at[0, 0, c],
            twin_sem.at[0, 1, c],
            {"half": other},
        )

    def twin_d(c, block):
        span = pl.ds(c * SPAN, SPAN)
        return remote(
            unit_d.at[block, span],
            unit_d.at[block, span],
            twin_sem.at[1, 0, c],
            twin_sem.at[1, 1, c],
            {"half": other},
        )

    def give_twin(c):
        twin_x(c, half).start()
        twin_d(c, half).start()

    def sum_copy(stage_no, c, way, src, dst):
        return remote(
            src,
            dst,
            sum_sem.at[stage_no, 0, way, c],
            sum_sem.at[stage_no, 1, way, c],
            {"dp": y_next if way == 0 else y_last},
        )

    def act_copy(stage_no, c, way, view):
        return remote(
            view,
            view,
            act_sem.at[stage_no, 0, way, c],
            act_sem.at[stage_no, 1, way, c],
            {"dp": y_next if way == 0 else y_last},
        )

    def columns(way):
        return pl.ds(way * mid, mid)

    def first_sum(c, way):
        return sum_copy(0, c, way, part.at[c, y_far, :, columns(way)], sum_one.at[c, way])

    def second_sum(c, way):
        toward = y_next if way == 0 else y_last
        return sum_copy(1, c, way, part.at[c, toward], sum_two.at[c, way])

    def select(c):
        twin_x(c, other).wait_recv()
        twin_d(c, other).wait_recv()
        span = pl.ds(c * SPAN, SPAN)
        block_x = [unit_x[b, span].reshape(SPAN * UNIT_TOK, width + LANES) for b in range(2)]
        all_x = jnp.concatenate(block_x, axis=0)
        is_expert = lax.broadcasted_iota(jnp.int32, (8, LANES), 1) == expert
        gate_row = matmul(is_expert.astype(BF16), all_x[:, width:], 1, 1)
        chosen = gate_row > 0.0
        rank = matmul(chosen.astype(BF16), before_chunk[...])
        place = jnp.where(chosen, slot_base[...] + rank, -1.0).astype(jnp.int32)
        row = lax.broadcasted_iota(jnp.int32, (SLOTS, TOKENS), 0)
        pick = (row == place[:1]).astype(BF16)
        gate_wide = matmul(
            pick, jnp.broadcast_to(gate_row[:1], (LANES, TOKENS)).astype(BF16), 1, 1
        )
        gates[c] = gate_wide
        slots = matmul(pick, all_x[:, :width]).astype(BF16)
        slot_x[c] = slots
        block_d = [unit_d[b, span].reshape(SPAN * UNIT_TOK, width) for b in range(2)]
        slots_d = matmul(pick, jnp.concatenate(block_d, axis=0))
        slot_s[c] = (gate_wide[:, :1] * slots_d).astype(BF16)
        shape = (NY, PART, hidden)
        part[c, :, :, 0:hidden] = matmul(slots, w_gate[...]).astype(BF16).reshape(shape)
        part[c, :, :, hidden : 2 * hidden] = matmul(slots, w_up[...]).astype(BF16).reshape(shape)
        part[c, :, :, 2 * hidden :] = (
            matmul(slots_d.astype(BF16), w_down[...]).astype(BF16).reshape(shape)
        )
        for way in range(2):
            first_sum(c, way).start()

    def add_passing(c):
        for way in range(2):
            first_sum(c, way).wait_recv()
            toward = y_next if way == 0 else y_last
            here = part[c, toward, :, columns(way)].astype(F32)
            part[c, toward, :, columns(way)] = (here + sum_one[c, way].astype(F32)).astype(BF16)
            second_sum(c, way).start()

    def activate(c):
        for way in range(2):
            second_sum(c, way).wait_recv()
        summed = (
            part[c, dp].astype(F32) + sum_two[c, 0].astype(F32) + sum_two[c, 1].astype(F32)
        )
        gate_act, up_act, back = (
            summed[:, :hidden],
            summed[:, hidden : 2 * hidden],
            summed[:, 2 * hidden :],
        )
        gate_col = gates[c, pl.ds(pl.multiple_of(dp * PART, PART), PART), :][:, :1]
        sigma = jax.nn.sigmoid(gate_act)
        active = gate_act * sigma
        slope = sigma * (1.0 + gate_act * (1.0 - sigma))
        units = (active * up_act).astype(BF16)
        scaled_back = gate_col * back
        act[c, dp, :, 0:hidden] = (scaled_back * up_act * slope).astype(BF16)
        act[c, dp, :, hidden : 2 * hidden] = (scaled_back * active).astype(BF16)
        act[c, dp, :, 2 * hidden :] = units
        route = jnp.sum(back * units.astype(F32), axis=1, keepdims=True)
        gates[c] = jnp.zeros((SLOTS, LANES), F32)
        gates[c, pl.ds(pl.multiple_of(dp * PART, PART), PART), :] = jnp.broadcast_to(
            route, (PART, LANES)
        )
        for way in range(2):
            act_copy(0, c, way, act.at[c, dp]).start()

    def pass_act(c):
        for way in range(2):
            source = y_last if way == 0 else y_next
            act_copy(0, c, way, act.at[c, source]).wait_recv()
            act_copy(1, c, way, act.at[c, source, :, columns(way)]).start()

    def half_copy(c):
        return remote(
            row_part.at[c, :, other],
            row_other.at[c],
            half_sem.at[0, c],
            half_sem.at[1, c],
            {"half": other},
        )

    def row_terms(c):
        for way in range(2):
            act_copy(1, c, way, act.at[c, y_far, :, columns(way)]).wait_recv()
        grads = act[c].reshape(SLOTS, three)
        rows = matmul(grads[:, :hidden], w_gate[...], 1, 1) + matmul(
            grads[:, hidden : 2 * hidden], w_up[...], 1, 1
        )
        row_part[c, :, :, :, 0:width] = rows.astype(BF16).reshape(SPAN, 2, UNIT, width)
        row_part[c, :, :, :, width:] = gates[c].astype(BF16).reshape(SPAN, 2, UNIT, LANES)
        half_copy(c).start()

    def back_copy(place, c, j, toward):
        return remote(
            row_send.at[c, j],
            row_back.at[expert],
            back_send.at[place],
            back_recv.at[expert],
            {"expert": toward},
        )

    def give_back(c):
        half_copy(c).wait_recv()
        for j in range(SPAN):
            place = c * SPAN + j
            row_send[c, j] = (
                row_part[c, j, half].astype(F32) + row_other[c, j].astype(F32)
            ).astype(BF16)
            step = div(place + 1, 2)
            offset = step + rem(place + 1, 2) * (RING - 2 * step)
            toward = ring_expert(rem(position + offset, RING), half)

            @pl.when(place != 0)
            def _():
                back_copy(place, c, j, toward).start()

            @pl.when(place == 0)
            def _():
                row_back[expert] = row_send[c, j]

    def weight_terms(c):
        def tile(m, carry):
            span = pl.ds(pl.multiple_of(m * LANES, LANES), LANES)
            acc[span, : 2 * hidden] += matmul(
                slot_x[c, :, span], act[c, :, :, : 2 * hidden].reshape(SLOTS, 2 * hidden), 0, 0
            )
            acc[span, 2 * hidden :] += matmul(
                slot_s[c, :, span], act[c, :, :, 2 * hidden :].reshape(SLOTS, hidden), 0, 0
            )
            return carry

        lax.fori_loop(0, width // LANES, tile, 0)

    def turn(i, carry):
        def staged(lag, work):
            pl.when((i >= lag) & (i - lag < CHUNKS))(functools.partial(work, i - lag))

        staged(0, lambda c: ring_step(2 * c + 1))
        staged(5, row_terms)
        staged(4, pass_act)
        staged(2, add_passing)
        staged(3, activate)

        @pl.when(i < CHUNKS)
        def _():
            ring_step(2 * i + 2)
            give_twin(i)

        staged(1, select)
        staged(6, give_back)
        staged(6, weight_terms)
        return carry

    lax.fori_loop(0, CHUNKS + 6, turn, 0)

    gate_out[...] = acc[:, :hidden].astype(BF16)
    up_out[...] = acc[:, hidden : 2 * hidden].astype(BF16)
    down_out[...] = acc[:, 2 * hidden :].astype(BF16)

    own_gate = own_rows[:, width : width + LANES]
    own_chosen = (own_gate.astype(F32) > 0.0).astype(BF16)
    own_rank = matmul(before_own[...], own_chosen).astype(BF16)
    chosen_at = matmul(own_chosen, spread[...])
    rank_at = matmul(own_rank, spread[...])
    combine = jnp.where(rank_at == slot_of[...], chosen_at, 0.0) * same_part[...]
    combine = combine.astype(BF16)

    def arrival(i, carry):
        source = rem(expert + i, RING)
        remote(
            row_send.at[0, 0],
            row_back.at[source],
            back_send.at[0],
            back_recv.at[source],
            {"expert": source},
        ).wait_recv()
        return carry

    lax.fori_loop(1, RING, arrival, 0)
    returned = row_back[...].reshape(RING * UNIT, width + LANES)
    token_sum = matmul(combine, returned[:, :width])
    route_sum = matmul(combine, returned[:, width:] * gather[...])
    fin_send[:, :, 0:width] = token_sum.astype(BF16).reshape(NY, PAD, width)
    fin_send[:, :, width:] = route_sum.astype(BF16).reshape(NY, PAD, LANES)

    def fin_copy(r):
        return remote(
            fin_send.at[rem(dp + r, NY)],
            fin_recv.at[dp],
            fin_sem.at[0, r],
            fin_sem.at[1, r],
            {"dp": rem(dp + r, NY)},
        )

    def fin_arrival(r):
        source = rem(dp + NY - r, NY)
        return remote(
            fin_send.at[source], fin_recv.at[source], fin_sem.at[0, r], fin_sem.at[1, r], {"dp": source}
        )

    for r in range(1, NY):
        fin_copy(r).start()
    fin_recv[dp] = fin_send[dp]
    for r in range(1, NY):
        fin_arrival(r).wait_recv()
    routes = jnp.zeros((PAD, LANES), F32)
    for q in range(NY):
        token_out[:, q * width : (q + 1) * width] = fin_recv[q, :, 0:width]
        routes = routes + fin_recv[q, :, width:].astype(F32)
    lane = lax.broadcasted_iota(jnp.int32, (PAD, LANES), 1)
    named = jnp.zeros((PAD, LANES), F32)
    for k in range(8):
        value = jnp.sum(jnp.where(ids[:, k : k + 1] == lane, routes, 0.0), axis=1, keepdims=True)
        named = jnp.where(lane == k, value, named)
    route_out[...] = named

    for r in range(1, NY):
        own_copy(r).wait_send()
        fin_copy(r).wait_send()

    def ring_left(step, carry):
        ring_x(step, behind, 0, 1).wait_send()
        ring_d(step, ahead, 0, 1).wait_send()

        @pl.when(step < LAST)
        def _():
            ring_x(step, ahead, 0, 1).wait_send()
            ring_d(step, behind, 0, 1).wait_send()

        return carry

    lax.fori_loop(1, LAST + 1, ring_left, 0)

    def chunk_left(c, carry):
        twin_x(c, half).wait_send()
        twin_d(c, half).wait_send()
        for way in range(2):
            first_sum(c, way).wait_send()
            second_sum(c, way).wait_send()
            act_copy(0, c, way, act.at[c, dp]).wait_send()
            act_copy(1, c, way, act.at[c, y_far, :, columns(way)]).wait_send()
        half_copy(c).wait_send()
        return carry

    lax.fori_loop(0, CHUNKS, chunk_left, 0)

    def back_left(place, carry):
        back_copy(place, 0, 0, ahead).wait_send()
        return carry

    lax.fori_loop(1, RING, back_left, 0)


def constants():
    n = np.arange(TOKENS)
    before_chunk = (n[:, None] // TOK == n[None] // TOK) & (n[:, None] < n[None])
    block, place, micro = n // (SPAN * UNIT_TOK), n // UNIT_TOK % SPAN, n // TOK % NY
    slot_base = np.broadcast_to((place * 2 + block) * UNIT + micro * MOST, (8, TOKENS))
    row, col = np.arange(UNIT_TOK), np.arange(NY * PAD)
    squeeze = (row[:, None] // TOK == col[None] // PAD) & (row[:, None] % TOK == col[None] % PAD)
    before_own = (col[:, None] // PAD == col[None] // PAD) & (col[None] < col[:, None])
    slot = np.arange(RING * UNIT)
    spread = np.arange(LANES)[:, None] == slot[None] // UNIT
    slot_of = np.broadcast_to(slot % MOST, (NY * PAD, RING * UNIT))
    same_part = col[:, None] // PAD == slot[None] // MOST % NY
    return (
        jnp.asarray(before_chunk, BF16),
        jnp.asarray(slot_base, F32),
        jnp.asarray(squeeze, BF16),
        jnp.asarray(before_own, BF16),
        jnp.asarray(spread, BF16),
        jnp.asarray(spread.T, BF16),
        jnp.asarray(slot_of, F32),
        jnp.asarray(same_part, F32),
    )


def on_device(tokens_in, cotangent, expert_ids, gate_probs, gate_weight, up_weight, down_weight):
    half = lax.axis_index("half")
    width, hidden = gate_weight.shape[1], gate_weight.shape[2]

    def block(values):
        return lax.dynamic_index_in_dim(values[0], half, 0, keepdims=False)

    def slices(values):
        return block(values).reshape(TOK, NY, width).transpose(1, 0, 2)

    ids = block(expert_ids)
    named = ids[:, :, None] == jnp.arange(LANES, dtype=jnp.int32)
    gate_map = jnp.sum(jnp.where(named, block(gate_probs).astype(F32)[:, :, None], 0.0), axis=1)
    gate_map = jnp.broadcast_to(gate_map.astype(BF16)[None], (NY, TOK, LANES))
    stage = jnp.concatenate([slices(tokens_in), gate_map, slices(cotangent)], axis=2)
    stage = jnp.pad(stage, ((0, 0), (0, PAD - TOK), (0, 0)))
    ids = jnp.pad(ids, ((0, PAD - TOK), (0, LANES - ids.shape[1])), constant_values=-1)

    vmem = pl.BlockSpec(memory_space=pltpu.VMEM)
    three = 3 * hidden
    weights = jax.ShapeDtypeStruct((width, hidden), BF16)
    out = pl.pallas_call(
        functools.partial(kernel, width, hidden),
        out_shape=(
            jax.ShapeDtypeStruct((PAD, NY * width), BF16),
            jax.ShapeDtypeStruct((PAD, LANES), F32),
            weights,
            weights,
            weights,
        ),
        in_specs=[vmem] * 13,
        out_specs=(vmem,) * 5,
        scratch_shapes=[
            pltpu.VMEM((NY, PAD, 2 * width + LANES), BF16),
            pltpu.VMEM((2, RING, UNIT_TOK, width + LANES), BF16),
            pltpu.VMEM((2, RING, UNIT_TOK, width), BF16),
            pltpu.VMEM((CHUNKS, SLOTS, width), BF16),
            pltpu.VMEM((CHUNKS, SLOTS, width), BF16),
            pltpu.VMEM((CHUNKS, SLOTS, LANES), F32),
            pltpu.VMEM((CHUNKS, NY, PART, three), BF16),
            pltpu.VMEM((CHUNKS, 2, PART, three // 2), BF16),
            pltpu.VMEM((CHUNKS, 2, PART, three), BF16),
            pltpu.VMEM((CHUNKS, NY, PART, three), BF16),
            pltpu.VMEM((CHUNKS, SPAN, 2, UNIT, width + LANES), BF16),
            pltpu.VMEM((CHUNKS, SPAN, UNIT, width + LANES), BF16),
            pltpu.VMEM((CHUNKS, SPAN, UNIT, width + LANES), BF16),
            pltpu.VMEM((RING, UNIT, width + LANES), BF16),
            pltpu.VMEM((NY, PAD, width + LANES), BF16),
            pltpu.VMEM((NY, PAD, width + LANES), BF16),
            pltpu.VMEM((width, three), F32),
            pltpu.SemaphoreType.DMA((2, NY)),
            pltpu.SemaphoreType.DMA((2, 2, 2, LAST)),
            pltpu.SemaphoreType.DMA((2, 2, CHUNKS)),
            pltpu.SemaphoreType.DMA((2, 2, 2, CHUNKS)),
            pltpu.SemaphoreType.DMA((2, 2, 2, CHUNKS)),
            pltpu.SemaphoreType.DMA((2, CHUNKS)),
            pltpu.SemaphoreType.DMA((RING,)),
            pltpu.SemaphoreType.DMA((RING,)),
            pltpu.SemaphoreType.DMA((2, NY)),
        ],
        compiler_params=pltpu.CompilerParams(
            collective_id=0, has_side_effects=True, vmem_limit_bytes=62 * 1024 * 1024
        ),
    )(stage, gate_weight[0], up_weight[0], down_weight[0], ids, *constants())
    token_rows, route_rows, gate_grad, up_grad, down_grad = out
    token_grad = token_rows[:TOK][None, None]
    route_grad = route_rows[:TOK, : expert_ids.shape[3]].astype(BF16)[None, None]
    return token_grad, route_grad, gate_grad[None], up_grad[None], down_grad[None]


def solution(mesh):
    return jax.shard_map(
        on_device,
        mesh=mesh,
        in_specs=(
            P(("expert", "dp"), None, None, None),
            P(("expert", "dp"), None, None, None),
            P(("expert", "dp"), None, None, None),
            P(("expert", "dp"), None, None, None),
            P("expert", "dp", "half"),
            P("expert", "dp", "half"),
            P("expert", "dp", "half"),
        ),
        out_specs=(
            P(("expert", "dp"), "half", None, None),
            P(("expert", "dp"), "half", None, None),
            P("expert", "dp", "half"),
            P("expert", "dp", "half"),
            P("expert", "dp", "half"),
        ),
        check_vma=False,
    )
```

time: 365 us -> 166 us (0.45)
  waiting for transfers between devices: 200 us -> 0 us
  Pallas kernels: 0 us -> 151 us
  local copies, waits for them, and re-layouts: 58.9 us -> 11.1 us
  starting transfers between devices: 38.5 us -> 0 us
  matrix products: 29.6 us -> 0 us
  other arithmetic: 19.2 us -> 0.85 us
  between operations: 14 us -> 0.7 us
    all_to_all x5 -> x0, waiting for transfers between devices: 162 us -> none  [the longest x1 57.5 us: on_device(): lax.all_to_all(send_dy.reshape(shaped + (model_width,)), 'expert', split_...]
    pallas_call x0 -> x1, Pallas kernels: none -> 151 us  [on_device(): pl.pallas_call(functools.partial(kernel, width, hidden), out_shape=(jax.S...]
    all_to_all x5 -> x0, starting transfers between devices: 37.9 us -> none  [the longest x1 11.6 us: on_device(): lax.all_to_all(send_gate.reshape(shaped), 'expert', split_axis=0, concat_...]
    unnamed x6 -> x0, waiting for transfers between devices: 37.9 us -> none
    dot_general x11 -> x0, matrix products: 29.6 us -> none  [the longest x1 5.33 us: expert_rows(): gate_act = jnp.dot(flat_x, w_gate, preferred_element_type=jnp.float32)]
    unnamed x27 -> x13, local copies, waits for them, and re-layouts: 26.1 us -> 5.97 us
    concatenate x1, other arithmetic: 14.9 us -> 0.74 us  [on_device(): jnp.concatenate([slices(tokens_in), gate_map, slices(cotangent)], axis=2)]
    reshape x4, local copies, waits for them, and re-layouts: 9.61 us -> 0.11 us  [slices(): return block(values).reshape(TOK, NY, width).transpose(1, 0, 2)]
  transfers between devices with their start and end apart: 10 -> 0, of which waited for: 6 -> 0; matrix products, arithmetic and copies ran while one was open for 23% -> 0% of each run, Pallas kernels for 0% -> 0%
where the time goes in v1:
time: 166 us; the launch traced here: 164 us
  Pallas kernels  151 us (91%)
  local copies, waits for them, and re-layouts  11.1 us (7%)
    pallas_call x1, Pallas kernels, on_device(): pl.pallas_call(functools.partial(kernel, width, hidden), out_shape=(jax.S...  151 us
    unnamed x13, local copies, waits for them, and re-layouts  5.97 us

profile of v1, /device:TPU:6, one launch (start us, length us, event | category | flops | bytes accessed | tf_op | source)
XLA Modules:
  0.0 164.1 jit_solution(12071547754070941655)
XLA Ops:
  0.6 0.0 copy-start
  0.7 0.7 copy-done
  1.3 0.0 copy-start.4
  1.3 0.1 copy.31
  1.4 0.6 copy-done.4
  2.0 0.1 copy.32
  2.1 0.1 select_reduce_fusion
  2.2 0.6 pad.9.ids
  2.8 2.1 %dynamic-slice_reduce_fusion = (bf16[12,3584]{1,0:T(8,128)(2,1)S(1)}, bf16[12,3584]{1,0:T(8,128)(2,1)S(1)}) fusion(bf16[1,2,12,3584]{3,1,2,0:T(2,128)(2,1)} %param.16, s32[]{:T(128)S(6)} %select_n.13, bf16[1,2,12,3584]{3,1,2,0:T(2,128)(2,1)} %param.15), kind=kLoop, calls=%fused_computation.6 | loop fusion | bytes 344068 | tf_op jit(solution)/shard_map/jit(dynamic_index_in_dim)/dynamic_slice | solution.py:550
  5.0 0.7 fusion.4.stage
  5.8 151.4 %shard_map.182 = (bf16[16,3584]{1,0:T(8,128)(2,1)}, f32[16,128]{1,0:T(8,128)}, bf16[896,512]{1,0:T(8,128)(2,1)}, bf16[896,512]{1,0:T(8,128)(2,1)}, bf16[896,512]{1,0:T(8,128)(2,1)}) custom-call(bf16[4,16,1920]{2,1,0:T(8,128)(2,1)} %fusion.4.stage, bf16[896,512]{1,0:T(8,128)(2,1)} %bitcast.23, bf16[896,512]{1,0:T(8,128)(2,1)} %bitcast.24, ...), custom_call_target="tpu_custom_call" | custom-call | tf_op jit(solution)/shard_map/pallas_call | solution.py:566
  157.2 0.0 copy-start.3
  157.2 1.6 slice_bitcast_fusion
  158.8 0.0 copy-done.3
  158.8 0.7 copy.35
  159.5 0.0 copy-start.2
  159.5 2.2 %copy.43 = bf16[1,896,512]{2,1,0:T(8,128)(2,1)} copy(bf16[1,896,512]{2,1,0:T(8,128)(2,1)} %bitcast.22) | data formatting | bytes 1835008
  161.7 0.0 copy-done.2
  161.7 0.0 copy-start.1
  161.7 0.9 copy.44
  162.6 0.6 copy-done.1
  163.2 0.9 copy.45
  (8 shorter events, 0.1 us)
Async XLA Ops:
  0.6 0.7 copy-start
  1.3 0.7 copy-start.4
  157.2 1.6 copy-start.3
  159.5 2.2 %copy-start.2 = (bf16[896,512]{1,0:T(8,128)(2,1)S(1)}, bf16[896,512]{1,0:T(8,128)(2,1)}, u32[]{:S(2)}) copy-start(bf16[896,512]{1,0:T(8,128)(2,1)} %get-tuple-element.13) | copy-start | bytes 2752516
  161.7 1.5 copy-start.1

commit v2 on v1

--- a/solution.py
+++ b/solution.py
@@ -2,7 +2,6 @@
 
 import jax
 import jax.numpy as jnp
-import numpy as np
 from jax import lax
 from jax.experimental import pallas as pl
 from jax.experimental.pallas import tpu as pltpu
@@ -17,8 +16,8 @@
 PAD = 16
 NX, NY, NZ = 4, 4, 8
 RING = NX * NZ
-LAST = RING // 2
-SPAN = 4
+LAST = NZ // 2
+SPAN = 2
 CHUNKS = RING // SPAN
 UNIT_TOK = NY * TOK
 UNIT = NY * MOST
@@ -36,19 +35,48 @@
     return lax.div(a, jnp.int32(b))
 
 
-def ring_position(expert, half):
+def choose(index, values):
+    found = jnp.int32(values[0])
+    for i, value in enumerate(values[1:], 1):
+        if value != values[0]:
+            found = jnp.where(index == i, jnp.int32(value), found)
+    return found
+
+
+Z_ORDER = (0, 1, 7, 2, 6, 3, 5, 4)
+FIRST_Z = (0, 0, 1, 7, 1, 7, 2, 6, 2, 6, 3, 5, 3, 5, 4, 4)
+FIRST_X = (0, 1, 0, 0, 1, 1, 0, 0, 1, 1, 0, 0, 1, 1, 0, 1)
+SECOND_X = (0, 0, 0, 0, 1, 3, 1, 3, 1, 3, 1, 3, 2, 2, 2, 2)
+SECOND_Z = (0, 1, 2, 3, 0, 0, 1, 1, 2, 2, 3, 3, 0, 1, 2, 3)
+
+
+def order(n):
+    return jnp.where(n < 4, n, jnp.where(n == CHUNKS - 1, 4, n + 1))
+
+
+def owner(expert, half, c, j):
     x, z = div(expert, NZ), rem(expert, NZ)
-    first = 4 * z + rem(x + z, 4)
-    turn = rem(z + 5 * x, NZ)
-    second = 4 * x + 16 * div(turn, 4) + rem(turn, 4)
+    first = rem(x + choose(c, FIRST_X) * SPAN + j, NX) * NZ + rem(z + choose(c, FIRST_Z), NZ)
+    z_step = choose(choose(c, SECOND_Z) * SPAN + j, Z_ORDER)
+    second = rem(x + choose(c, SECOND_X), NX) * NZ + rem(z + z_step, NZ)
     return first + half * (second - first)
 
 
-def ring_expert(position, half):
-    group, inner = div(position, 4), rem(position, 4)
-    first = rem(inner + 3 * group, NX) * NZ + group
-    second = rem(group, NX) * NZ + rem(3 * group + inner, NZ)
-    return first + half * (second - first)
+def index_of(shape, dim):
+    return lax.broadcasted_iota(jnp.int32, shape, dim).astype(F32)
+
+
+def whole(number, size):
+    return jnp.floor((number + 0.5) * (1.0 / size))
+
+
+def part_of(number, size):
+    return number - size * whole(number, size)
+
+
+def before(size, span):
+    row, col = index_of((size, size), 0), index_of((size, size), 1)
+    return jnp.where((whole(row, span) == whole(col, span)) & (row < col), 1.0, 0.0).astype(BF16)
 
 
 def matmul(a, b, a_dim=1, b_dim=0):
@@ -59,23 +87,17 @@
     width,
     hidden,
     stage,
+    w_gate_hbm,
+    w_up_hbm,
+    w_down_hbm,
+    ids,
+    token_out,
+    route_out,
+    grads_hbm,
     w_gate,
     w_up,
     w_down,
-    ids,
     before_chunk,
-    slot_base,
-    squeeze,
-    before_own,
-    spread,
-    gather,
-    slot_of,
-    same_part,
-    token_out,
-    route_out,
-    gate_out,
-    up_out,
-    down_out,
     own,
     unit_x,
     unit_d,
@@ -93,8 +115,10 @@
     fin_send,
     fin_recv,
     acc,
+    grads_out,
     own_sem,
-    ring_sem,
+    near_sem,
+    far_sem,
     twin_sem,
     sum_sem,
     act_sem,
@@ -102,12 +126,20 @@
     back_send,
     back_recv,
     fin_sem,
+    load_sem,
 ):
+    loads = [
+        pltpu.make_async_copy(src, dst, load_sem.at[n])
+        for n, (src, dst) in enumerate(((w_gate_hbm, w_gate), (w_up_hbm, w_up), (w_down_hbm, w_down)))
+    ]
+    for load in loads:
+        load.start()
     expert, half, dp = lax.axis_index("expert"), lax.axis_index("half"), lax.axis_index("dp")
     other = 1 - half
-    position = ring_position(expert, half)
-    ahead = ring_expert(rem(position + 1, RING), half)
-    behind = ring_expert(rem(position + RING - 1, RING), half)
+    x, z = div(expert, NZ), rem(expert, NZ)
+    z_next, z_last = x * NZ + rem(z + 1, NZ), x * NZ + rem(z + NZ - 1, NZ)
+    z_two_next, z_two_last = x * NZ + rem(z + 2, NZ), x * NZ + rem(z + NZ - 2, NZ)
+    x_at = [rem(x + r, NX) * NZ + z for r in range(NX)]
     y_next, y_last, y_far = rem(dp + 1, NY), rem(dp + 3, NY), rem(dp + 2, NY)
     three = 3 * hidden
     mid = three // 2
@@ -129,6 +161,12 @@
     for r in range(1, NY):
         pl.semaphore_signal(barrier, inc=1, device_id={"dp": rem(dp + r, NY)}, device_id_type=MESH)
     pl.semaphore_signal(barrier, inc=1, device_id={"half": other}, device_id_type=MESH)
+    acc[...] = jnp.zeros_like(acc)
+    before_chunk[...] = before(TOKENS, TOK)
+    own[dp] = stage[dp]
+    row, col = index_of((UNIT_TOK, NY * PAD), 0), index_of((UNIT_TOK, NY * PAD), 1)
+    same = (whole(row, TOK) == whole(col, PAD)) & (part_of(row, TOK) == part_of(col, PAD))
+    squeeze = jnp.where(same, 1.0, 0.0).astype(BF16)
     pl.semaphore_wait(barrier, RING - 1 + NY - 1 + 1)
 
     def own_copy(r):
@@ -146,71 +184,141 @@
 
     for r in range(1, NY):
         own_copy(r).start()
-    own[dp] = stage[dp]
-    acc[...] = jnp.zeros_like(acc)
     for r in range(1, NY):
         own_arrival(r).wait_recv()
     own_rows = own[...].reshape(NY * PAD, 2 * width + LANES)
-    packed = matmul(squeeze[...], own_rows).astype(BF16)
+    packed = matmul(squeeze, own_rows).astype(BF16)
     unit_x[half, 0] = packed[:, : width + LANES]
     unit_d[half, 0] = packed[:, width + LANES :]
 
-    def ring_x(step, toward, src, dst):
-        way = 0 if toward is ahead else 1
-        return remote(
-            unit_x.at[half, src],
-            unit_x.at[half, dst],
-            ring_sem.at[0, 0, way, step - 1],
-            ring_sem.at[0, 1, way, step - 1],
+    units = (unit_x, unit_d)
+
+    def near(kind, src, dst, toward):
+        return remote(
+            units[kind].at[half, src],
+            units[kind].at[half, dst],
+            near_sem.at[kind, 0, dst],
+            near_sem.at[kind, 1, dst],
             {"expert": toward},
         )
 
-    def ring_d(step, toward, src, dst):
-        way = 0 if toward is ahead else 1
-        return remote(
-            unit_d.at[half, src],
-            unit_d.at[half, dst],
-            ring_sem.at[1, 0, way, step - 1],
-            ring_sem.at[1, 1, way, step - 1],
+    def far(kind, src, dst, toward):
+        return remote(
+            units[kind].at[half, pl.ds(src * SPAN, SPAN)],
+            units[kind].at[half, pl.ds(dst * SPAN, SPAN)],
+            far_sem.at[kind, 0, dst],
+            far_sem.at[kind, 1, dst],
             {"expert": toward},
         )
 
-    ring_x(1, ahead, 0, 2).start()
-    ring_x(1, behind, 0, 1).start()
-    ring_d(1, ahead, 0, 2).start()
-    ring_d(1, behind, 0, 1).start()
-
-    def ring_step(step):
-        fore, aft = 2 * step - 1, 2 * step
-        more, inner = step + 1 < LAST, step < LAST
-        ring_x(step, behind, fore, fore).wait_recv()
-
-        @pl.when(inner)
-        def _():
-            ring_x(step + 1, behind, fore, fore + 2).start()
-            ring_d(step, behind, fore, fore).wait_recv()
-            ring_x(step, ahead, aft, aft).wait_recv()
-
-        @pl.when(more)
-        def _():
-            ring_d(step + 1, behind, fore, fore + 2).start()
-            ring_x(step + 1, ahead, aft, aft + 2).start()
-
-        @pl.when(inner)
-        def _():
-            ring_d(step, ahead, aft, aft).wait_recv()
-
-        @pl.when(more)
-        def _():
-            ring_d(step + 1, ahead, aft, aft + 2).start()
-
-        @pl.when(step == LAST - 1)
-        def _():
-            ring_d(step + 1, ahead, aft, fore + 2).start()
-
-        @pl.when(step == LAST)
-        def _():
-            ring_d(step, ahead, fore, fore).wait_recv()
+    def near_wait(dst):
+        for kind in range(2):
+            near(kind, dst, dst, z_next).wait_recv()
+
+    def near_pass(src, dst, toward):
+        for kind in range(2):
+            near(kind, src, dst, toward).start()
+
+    def far_wait(dst):
+        for kind in range(2):
+            far(kind, dst, dst, z_next).wait_recv()
+
+    def far_pass(src, dst, toward):
+        for kind in range(2):
+            far(kind, src, dst, toward).start()
+
+    @pl.when(half == 0)
+    def _():
+        near_pass(0, 1, x_at[3])
+        near_pass(0, 3, x_at[1])
+
+    @pl.when(half == 1)
+    def _():
+        near_pass(0, 1, z_last)
+        near_pass(0, 2, z_next)
+
+    def take_first(c):
+        @pl.when(c == 0)
+        def _():
+            near_wait(1)
+            near_pass(0, 2, x_at[2])
+
+        @pl.when(c == 1)
+        def _():
+            near_wait(3)
+            near_wait(2)
+
+        @pl.when(c > 1)
+        def _():
+            far_wait(c)
+
+        @pl.when(c < 2)
+        def _():
+            far_pass(c, 2 * c + 2, z_last)
+            far_pass(c, 2 * c + 3, z_next)
+
+        even = rem(c, 2) == 0
+
+        @pl.when((c > 1) & (c < 11) & even)
+        def _():
+            far_pass(c, c + 4, z_last)
+
+        @pl.when((c > 1) & (c < 10) & jnp.logical_not(even))
+        def _():
+            far_pass(c, c + 4, z_next)
+
+        @pl.when(c == 13)
+        def _():
+            far_pass(c, 15, z_next)
+
+    def take_second(c):
+        @pl.when(c == 0)
+        def _():
+            near_wait(1)
+            near_pass(0, 3, z_two_last)
+            near_pass(0, 4, z_two_next)
+
+        @pl.when(c == 1)
+        def _():
+            near_wait(2)
+            near_wait(3)
+            near_pass(3, 5, z_last)
+
+        @pl.when(c == 2)
+        def _():
+            near_wait(4)
+            near_pass(4, 6, z_next)
+            near_wait(5)
+            near(0, 5, 7, z_last).start()
+
+        @pl.when(c == 3)
+        def _():
+            near_wait(6)
+            near(1, 6, 7, z_next).start()
+            near_wait(7)
+
+        @pl.when(c > 3)
+        def _():
+            far_wait(c)
+
+        @pl.when(c < 4)
+        def _():
+            far_pass(c, 2 * c + 4, x_at[3])
+            far_pass(c, 2 * c + 5, x_at[1])
+
+        @pl.when((c == 4) | (c == 6))
+        def _():
+            far_pass(c, 10 + div(c, 2), x_at[3])
+
+        @pl.when((c == 9) | (c == 11))
+        def _():
+            far_pass(c, 10 + div(c, 2), x_at[1])
+
+    def take(c):
+        pl.when(half == 0)(functools.partial(take_first, c))
+        pl.when(half == 1)(functools.partial(take_second, c))
+        twin_x(c, half).start()
+        twin_d(c, half).start()
 
     def twin_x(c, block):
         span = pl.ds(c * SPAN, SPAN)
@@ -232,10 +340,6 @@
             {"half": other},
         )
 
-    def give_twin(c):
-        twin_x(c, half).start()
-        twin_d(c, half).start()
-
     def sum_copy(stage_no, c, way, src, dst):
         return remote(
             src,
@@ -265,18 +369,22 @@
         return sum_copy(1, c, way, part.at[c, toward], sum_two.at[c, way])
 
     def select(c):
-        twin_x(c, other).wait_recv()
-        twin_d(c, other).wait_recv()
-        span = pl.ds(c * SPAN, SPAN)
+        chunk = order(c)
+        twin_x(chunk, other).wait_recv()
+        twin_d(chunk, other).wait_recv()
+        span = pl.ds(chunk * SPAN, SPAN)
         block_x = [unit_x[b, span].reshape(SPAN * UNIT_TOK, width + LANES) for b in range(2)]
         all_x = jnp.concatenate(block_x, axis=0)
         is_expert = lax.broadcasted_iota(jnp.int32, (8, LANES), 1) == expert
         gate_row = matmul(is_expert.astype(BF16), all_x[:, width:], 1, 1)
         chosen = gate_row > 0.0
         rank = matmul(chosen.astype(BF16), before_chunk[...])
-        place = jnp.where(chosen, slot_base[...] + rank, -1.0).astype(jnp.int32)
-        row = lax.broadcasted_iota(jnp.int32, (SLOTS, TOKENS), 0)
-        pick = (row == place[:1]).astype(BF16)
+        token = index_of((8, TOKENS), 1)
+        unit = whole(token, UNIT_TOK)
+        unit = part_of(unit, SPAN) * 2 + whole(unit, SPAN)
+        base = unit * UNIT + part_of(whole(token, TOK), NY) * MOST
+        place = jnp.where(chosen, base + rank, -1.0)
+        pick = jnp.where(index_of((SLOTS, TOKENS), 0) == place[:1], 1.0, 0.0).astype(BF16)
         gate_wide = matmul(
             pick, jnp.broadcast_to(gate_row[:1], (LANES, TOKENS)).astype(BF16), 1, 1
         )
@@ -373,9 +481,7 @@
             row_send[c, j] = (
                 row_part[c, j, half].astype(F32) + row_other[c, j].astype(F32)
             ).astype(BF16)
-            step = div(place + 1, 2)
-            offset = step + rem(place + 1, 2) * (RING - 2 * step)
-            toward = ring_expert(rem(position + offset, RING), half)
+            toward = owner(expert, half, order(c), j)
 
             @pl.when(place != 0)
             def _():
@@ -386,51 +492,71 @@
                 row_back[expert] = row_send[c, j]
 
     def weight_terms(c):
+        pair = pl.ds(c - 1, 2)
+
         def tile(m, carry):
             span = pl.ds(pl.multiple_of(m * LANES, LANES), LANES)
             acc[span, : 2 * hidden] += matmul(
-                slot_x[c, :, span], act[c, :, :, : 2 * hidden].reshape(SLOTS, 2 * hidden), 0, 0
+                slot_x[pair, :, span].reshape(2 * SLOTS, LANES),
+                act[pair, :, :, : 2 * hidden].reshape(2 * SLOTS, 2 * hidden),
+                0,
+                0,
             )
             acc[span, 2 * hidden :] += matmul(
-                slot_s[c, :, span], act[c, :, :, 2 * hidden :].reshape(SLOTS, hidden), 0, 0
+                slot_s[pair, :, span].reshape(2 * SLOTS, LANES),
+                act[pair, :, :, 2 * hidden :].reshape(2 * SLOTS, hidden),
+                0,
+                0,
             )
             return carry
 
-        lax.fori_loop(0, width // LANES, tile, 0)
+        @pl.when(rem(c, 2) == 1)
+        def _():
+            lax.fori_loop(0, width // LANES, tile, 0)
+
+    for load in loads:
+        load.wait()
 
     def turn(i, carry):
         def staged(lag, work):
             pl.when((i >= lag) & (i - lag < CHUNKS))(functools.partial(work, i - lag))
 
-        staged(0, lambda c: ring_step(2 * c + 1))
-        staged(5, row_terms)
-        staged(4, pass_act)
-        staged(2, add_passing)
-        staged(3, activate)
-
-        @pl.when(i < CHUNKS)
-        def _():
-            ring_step(2 * i + 2)
-            give_twin(i)
-
+        staged(7, pass_act)
+        staged(5, activate)
+        staged(3, add_passing)
         staged(1, select)
-        staged(6, give_back)
-        staged(6, weight_terms)
+        first = i + jnp.where(i > 4, 1, 0)
+        beyond = jnp.minimum(i + 1 + jnp.where(i > 3, 1, 0), CHUNKS)
+
+        def take_one(c, carry):
+            take(c)
+            return carry
+
+        lax.fori_loop(first, beyond, take_one, 0)
+        staged(9, row_terms)
+        staged(10, give_back)
+        staged(11, weight_terms)
         return carry
 
-    lax.fori_loop(0, CHUNKS + 6, turn, 0)
-
-    gate_out[...] = acc[:, :hidden].astype(BF16)
-    up_out[...] = acc[:, hidden : 2 * hidden].astype(BF16)
-    down_out[...] = acc[:, 2 * hidden :].astype(BF16)
+    lax.fori_loop(0, CHUNKS + 11, turn, 0)
 
     own_gate = own_rows[:, width : width + LANES]
     own_chosen = (own_gate.astype(F32) > 0.0).astype(BF16)
-    own_rank = matmul(before_own[...], own_chosen).astype(BF16)
-    chosen_at = matmul(own_chosen, spread[...])
-    rank_at = matmul(own_rank, spread[...])
-    combine = jnp.where(rank_at == slot_of[...], chosen_at, 0.0) * same_part[...]
-    combine = combine.astype(BF16)
+    own_rank = matmul(before(NY * PAD, PAD), own_chosen, 0, 0).astype(BF16)
+    returns = RING * UNIT
+    spread = jnp.where(
+        index_of((LANES, returns), 0) == whole(index_of((LANES, returns), 1), UNIT), 1.0, 0.0
+    ).astype(BF16)
+    chosen_at = matmul(own_chosen, spread)
+    rank_at = matmul(own_rank, spread)
+    own_token, slot = index_of((NY * PAD, returns), 0), index_of((NY * PAD, returns), 1)
+    fits = (rank_at == part_of(slot, MOST)) & (
+        whole(own_token, PAD) == part_of(whole(slot, MOST), NY)
+    )
+    combine = jnp.where(fits, chosen_at, 0.0).astype(BF16)
+    gather = jnp.where(
+        whole(index_of((returns, LANES), 0), UNIT) == index_of((returns, LANES), 1), 1.0, 0.0
+    ).astype(BF16)
 
     def arrival(i, carry):
         source = rem(expert + i, RING)
@@ -446,7 +572,7 @@
     lax.fori_loop(1, RING, arrival, 0)
     returned = row_back[...].reshape(RING * UNIT, width + LANES)
     token_sum = matmul(combine, returned[:, :width])
-    route_sum = matmul(combine, returned[:, width:] * gather[...])
+    route_sum = matmul(combine, returned[:, width:] * gather)
     fin_send[:, :, 0:width] = token_sum.astype(BF16).reshape(NY, PAD, width)
     fin_send[:, :, width:] = route_sum.astype(BF16).reshape(NY, PAD, LANES)
 
@@ -468,6 +594,10 @@
     for r in range(1, NY):
         fin_copy(r).start()
     fin_recv[dp] = fin_send[dp]
+    for n in range(3):
+        grads_out[n] = acc[:, n * hidden : (n + 1) * hidden].astype(BF16)
+    store = pltpu.make_async_copy(grads_out, grads_hbm, load_sem.at[3])
+    store.start()
     for r in range(1, NY):
         fin_arrival(r).wait_recv()
     routes = jnp.zeros((PAD, LANES), F32)
@@ -481,22 +611,27 @@
         named = jnp.where(lane == k, value, named)
     route_out[...] = named
 
+    store.wait()
     for r in range(1, NY):
         own_copy(r).wait_send()
         fin_copy(r).wait_send()
 
-    def ring_left(step, carry):
-        ring_x(step, behind, 0, 1).wait_send()
-        ring_d(step, ahead, 0, 1).wait_send()
-
-        @pl.when(step < LAST)
-        def _():
-            ring_x(step, ahead, 0, 1).wait_send()
-            ring_d(step, behind, 0, 1).wait_send()
-
-        return carry
-
-    lax.fori_loop(1, LAST + 1, ring_left, 0)
+    for kind in range(2):
+        for dst in range(1, NX):
+            near(kind, 0, dst, z_next).wait_send()
+
+        @pl.when(half == 0)
+        def _(kind=kind):
+            far(kind, 0, 2, z_next).wait_send()
+            far(kind, 0, 3, z_next).wait_send()
+
+        @pl.when(half == 1)
+        def _(kind=kind):
+            for dst in range(NX, NZ):
+                near(kind, 0, dst, z_next).wait_send()
+
+        for dst in range(4, CHUNKS):
+            far(kind, 0, dst, z_next).wait_send()
 
     def chunk_left(c, carry):
         twin_x(c, half).wait_send()
@@ -512,34 +647,23 @@
     lax.fori_loop(0, CHUNKS, chunk_left, 0)
 
     def back_left(place, carry):
-        back_copy(place, 0, 0, ahead).wait_send()
+        back_copy(place, 0, 0, z_next).wait_send()
         return carry
 
     lax.fori_loop(1, RING, back_left, 0)
 
 
-def constants():
-    n = np.arange(TOKENS)
-    before_chunk = (n[:, None] // TOK == n[None] // TOK) & (n[:, None] < n[None])
-    block, place, micro = n // (SPAN * UNIT_TOK), n // UNIT_TOK % SPAN, n // TOK % NY
-    slot_base = np.broadcast_to((place * 2 + block) * UNIT + micro * MOST, (8, TOKENS))
-    row, col = np.arange(UNIT_TOK), np.arange(NY * PAD)
-    squeeze = (row[:, None] // TOK == col[None] // PAD) & (row[:, None] % TOK == col[None] % PAD)
-    before_own = (col[:, None] // PAD == col[None] // PAD) & (col[None] < col[:, None])
-    slot = np.arange(RING * UNIT)
-    spread = np.arange(LANES)[:, None] == slot[None] // UNIT
-    slot_of = np.broadcast_to(slot % MOST, (NY * PAD, RING * UNIT))
-    same_part = col[:, None] // PAD == slot[None] // MOST % NY
-    return (
-        jnp.asarray(before_chunk, BF16),
-        jnp.asarray(slot_base, F32),
-        jnp.asarray(squeeze, BF16),
-        jnp.asarray(before_own, BF16),
-        jnp.asarray(spread, BF16),
-        jnp.asarray(spread.T, BF16),
-        jnp.asarray(slot_of, F32),
-        jnp.asarray(same_part, F32),
-    )
+def finish(token_rows, route_rows, grads, token_out, route_out, gate_out, up_out, down_out, sem):
+    copies = [
+        pltpu.make_async_copy(grads.at[n], target.at[0], sem.at[n])
+        for n, target in enumerate((gate_out, up_out, down_out))
+    ]
+    for copy in copies:
+        copy.start()
+    token_out[0, 0] = token_rows[:TOK]
+    route_out[0, 0] = route_rows[:TOK, : route_out.shape[3]].astype(BF16)
+    for copy in copies:
+        copy.wait()
 
 
 def on_device(tokens_in, cotangent, expert_ids, gate_probs, gate_weight, up_weight, down_weight):
@@ -547,7 +671,7 @@
     width, hidden = gate_weight.shape[1], gate_weight.shape[2]
 
     def block(values):
-        return lax.dynamic_index_in_dim(values[0], half, 0, keepdims=False)
+        return jnp.where(half == 0, values[0, 0], values[0, 1])
 
     def slices(values):
         return block(values).reshape(TOK, NY, width).transpose(1, 0, 2)
@@ -561,20 +685,21 @@
     ids = jnp.pad(ids, ((0, PAD - TOK), (0, LANES - ids.shape[1])), constant_values=-1)
 
     vmem = pl.BlockSpec(memory_space=pltpu.VMEM)
+    hbm = pl.BlockSpec(memory_space=pl.ANY)
     three = 3 * hidden
-    weights = jax.ShapeDtypeStruct((width, hidden), BF16)
+    weights = jax.ShapeDtypeStruct((1, width, hidden), BF16)
     out = pl.pallas_call(
         functools.partial(kernel, width, hidden),
         out_shape=(
             jax.ShapeDtypeStruct((PAD, NY * width), BF16),
             jax.ShapeDtypeStruct((PAD, LANES), F32),
-            weights,
-            weights,
-            weights,
+            jax.ShapeDtypeStruct((3, width, hidden), BF16),
         ),
-        in_specs=[vmem] * 13,
-        out_specs=(vmem,) * 5,
+        in_specs=[vmem] + [hbm] * 3 + [vmem],
+        out_specs=(vmem, vmem, hbm),
         scratch_shapes=[
+            *[pltpu.VMEM((width, hidden), BF16)] * 3,
+            pltpu.VMEM((TOKENS, TOKENS), BF16),
             pltpu.VMEM((NY, PAD, 2 * width + LANES), BF16),
             pltpu.VMEM((2, RING, UNIT_TOK, width + LANES), BF16),
             pltpu.VMEM((2, RING, UNIT_TOK, width), BF16),
@@ -592,8 +717,10 @@
             pltpu.VMEM((NY, PAD, width + LANES), BF16),
             pltpu.VMEM((NY, PAD, width + LANES), BF16),
             pltpu.VMEM((width, three), F32),
+            pltpu.VMEM((3, width, hidden), BF16),
             pltpu.SemaphoreType.DMA((2, NY)),
-            pltpu.SemaphoreType.DMA((2, 2, 2, LAST)),
+            pltpu.SemaphoreType.DMA((2, 2, NZ)),
+            pltpu.SemaphoreType.DMA((2, 2, CHUNKS)),
             pltpu.SemaphoreType.DMA((2, 2, CHUNKS)),
             pltpu.SemaphoreType.DMA((2, 2, 2, CHUNKS)),
             pltpu.SemaphoreType.DMA((2, 2, 2, CHUNKS)),
@@ -601,15 +728,25 @@
             pltpu.SemaphoreType.DMA((RING,)),
             pltpu.SemaphoreType.DMA((RING,)),
             pltpu.SemaphoreType.DMA((2, NY)),
+            pltpu.SemaphoreType.DMA((4,)),
         ],
         compiler_params=pltpu.CompilerParams(
             collective_id=0, has_side_effects=True, vmem_limit_bytes=62 * 1024 * 1024
         ),
-    )(stage, gate_weight[0], up_weight[0], down_weight[0], ids, *constants())
-    token_rows, route_rows, gate_grad, up_grad, down_grad = out
-    token_grad = token_rows[:TOK][None, None]
-    route_grad = route_rows[:TOK, : expert_ids.shape[3]].astype(BF16)[None, None]
-    return token_grad, route_grad, gate_grad[None], up_grad[None], down_grad[None]
+    )(stage, gate_weight[0], up_weight[0], down_weight[0], ids)
+    return pl.pallas_call(
+        finish,
+        out_shape=(
+            jax.ShapeDtypeStruct((1, 1, TOK, NY * width), BF16),
+            jax.ShapeDtypeStruct((1, 1, TOK, expert_ids.shape[3]), BF16),
+            weights,
+            weights,
+            weights,
+        ),
+        in_specs=[vmem, vmem, hbm],
+        out_specs=(vmem, vmem, hbm, hbm, hbm),
+        scratch_shapes=[pltpu.SemaphoreType.DMA((3,))],
+    )(*out)
 
 
 def solution(mesh):

time: 166 us -> 235 us (1.42)
  Pallas kernels: 151 us -> 225 us
  local copies, waits for them, and re-layouts: 11.1 us -> 2.22 us
  other arithmetic: 0.85 us -> 4.46 us
    pallas_call x0 -> x1, Pallas kernels: none -> 86.1 us  [on_device(): pl.pallas_call(finish, out_shape=(jax.ShapeDtypeStruct((1, 1, TOK, NY * w...]
    pallas_call x1, Pallas kernels: 151 us -> 139 us  [on_device(): pl.pallas_call(functools.partial(kernel, width, hidden), out_shape=(jax.S...]
    unnamed x13 -> x0, local copies, waits for them, and re-layouts: 5.97 us -> none
    select_n x0 -> x2, other arithmetic: none -> 2.91 us  [block(): return jnp.where(half == 0, values[0, 0], values[0, 1])]
where the time goes in v2:
time: 235 us; the launch traced here: 233 us
  Pallas kernels  225 us (96%)
  other arithmetic  4.46 us (2%)
    pallas_call x1, Pallas kernels, on_device(): pl.pallas_call(functools.partial(kernel, width, hidden), out_shape=(jax.S...  139 us
    pallas_call x1, Pallas kernels, on_device(): pl.pallas_call(finish, out_shape=(jax.ShapeDtypeStruct((1, 1, TOK, NY * w...  86.1 us

profile of v2, /device:TPU:6, one launch (start us, length us, event | category | flops | bytes accessed | tf_op | source)
XLA Modules:
  0.0 232.8 jit_solution(17879203633708301772)
XLA Ops:
  0.6 0.7 select_bitcast_fusion
  1.3 0.1 copy.23
  1.4 0.7 bitcast_convert_fusion
  2.1 0.1 copy.24
  2.2 0.1 select_reduce_fusion
  2.3 0.6 pad.9.ids
  2.9 2.2 fusion.5
  5.3 0.7 fusion.4.stage
  6.0 139.4 %shard_map.110 = (bf16[16,3584]{1,0:T(8,128)(2,1)}, f32[16,128]{1,0:T(8,128)}, bf16[3,896,512]{2,1,0:T(8,128)(2,1)}) custom-call(bf16[4,16,1920]{2,1,0:T(8,128)(2,1)} %fusion.4.stage, bf16[896,512]{1,0:T(8,128)(2,1)} %bitcast.14, bf16[896,512]{1,0:T(8,128)(2,1)} %bitcast.15, bf16[896,512]{1,0:T(8,128)(2,1)} %bitcast.16, s32[16,128]{1,0:T(8,128)} %pad.9.ids), custom_call_target="tpu_custom_call" | custom-call | tf_op jit(solution)/shard_map/pallas_call | solution.py:691
  145.4 86.1 %shard_map.111 = (bf16[1,1,12,3584]{3,2,1,0:T(8,128)(2,1)}, bf16[1,1,12,8]{3,2,1,0:T(8,128)(2,1)}, bf16[1,896,512]{2,1,0:T(8,128)(2,1)}, bf16[1,896,512]{2,1,0:T(8,128)(2,1)}, bf16[1,896,512]{2,1,0:T(8,128)(2,1)}) custom-call(bf16[16,3584]{1,0:T(8,128)(2,1)} %get-tuple-element.8.token_rows, f32[16,128]{1,0:T(8,128)} %get-tuple-element.9.route_rows, ...), custom_call_target="tpu_custom_call" | custom-call | tf_op jit(solution)/shard_map/pallas_call | solution.py:737
  231.5 1.3 copy.27
  (5 shorter events, 0.1 us)

commit v3 on v2

--- a/solution.py
+++ b/solution.py
@@ -11,6 +11,7 @@
 BF16 = jnp.bfloat16
 F32 = jnp.float32
 
+TOP = 8
 MOST = 6
 TOK = 12
 PAD = 16
@@ -86,11 +87,13 @@
 def kernel(
     width,
     hidden,
-    stage,
+    tokens,
+    cotangent,
+    ids,
+    probs,
     w_gate_hbm,
     w_up_hbm,
     w_down_hbm,
-    ids,
     token_out,
     route_out,
     grads_hbm,
@@ -98,9 +101,9 @@
     w_up,
     w_down,
     before_chunk,
+    stage,
     own,
-    unit_x,
-    unit_d,
+    units,
     slot_x,
     slot_s,
     gates,
@@ -163,6 +166,21 @@
     pl.semaphore_signal(barrier, inc=1, device_id={"half": other}, device_id_type=MESH)
     acc[...] = jnp.zeros_like(acc)
     before_chunk[...] = before(TOKENS, TOK)
+    row, col = index_of((PAD, 2 * TOK), 0), index_of((PAD, 2 * TOK), 1)
+    mine = jnp.where((row < TOK) & (col == 2 * row + half), 1.0, 0.0).astype(BF16)
+    block_x = matmul(mine, tokens[...].reshape(2 * TOK, NY * width)).astype(BF16)
+    block_d = matmul(mine, cotangent[...].reshape(2 * TOK, NY * width)).astype(BF16)
+    named, weight = ids[half], probs[half].astype(F32)
+    lane = lax.broadcasted_iota(jnp.int32, (LANES, TOK), 0)
+    gate_map = jnp.zeros((LANES, TOK), F32)
+    for k in range(TOP):
+        gate_map = jnp.where(named[k : k + 1] == lane, weight[k : k + 1], gate_map)
+    unit = jnp.where(index_of((PAD, TOK), 0) == index_of((PAD, TOK), 1), 1.0, 0.0).astype(BF16)
+    gate_map = matmul(unit, gate_map.astype(BF16), 1, 1).astype(BF16)
+    for q in range(NY):
+        stage[q, :, 0:width] = block_x[:, q * width : (q + 1) * width]
+        stage[q, :, width : width + LANES] = gate_map
+        stage[q, :, width + LANES :] = block_d[:, q * width : (q + 1) * width]
     own[dp] = stage[dp]
     row, col = index_of((UNIT_TOK, NY * PAD), 0), index_of((UNIT_TOK, NY * PAD), 1)
     same = (whole(row, TOK) == whole(col, PAD)) & (part_of(row, TOK) == part_of(col, PAD))
@@ -188,44 +206,37 @@
         own_arrival(r).wait_recv()
     own_rows = own[...].reshape(NY * PAD, 2 * width + LANES)
     packed = matmul(squeeze, own_rows).astype(BF16)
-    unit_x[half, 0] = packed[:, : width + LANES]
-    unit_d[half, 0] = packed[:, width + LANES :]
-
-    units = (unit_x, unit_d)
-
-    def near(kind, src, dst, toward):
-        return remote(
-            units[kind].at[half, src],
-            units[kind].at[half, dst],
-            near_sem.at[kind, 0, dst],
-            near_sem.at[kind, 1, dst],
+    units[half, 0] = packed
+
+    def near(src, dst, toward):
+        return remote(
+            units.at[half, src],
+            units.at[half, dst],
+            near_sem.at[0, dst],
+            near_sem.at[1, dst],
             {"expert": toward},
         )
 
-    def far(kind, src, dst, toward):
-        return remote(
-            units[kind].at[half, pl.ds(src * SPAN, SPAN)],
-            units[kind].at[half, pl.ds(dst * SPAN, SPAN)],
-            far_sem.at[kind, 0, dst],
-            far_sem.at[kind, 1, dst],
+    def far(src, dst, toward):
+        return remote(
+            units.at[half, pl.ds(src * SPAN, SPAN)],
+            units.at[half, pl.ds(dst * SPAN, SPAN)],
+            far_sem.at[0, dst],
+            far_sem.at[1, dst],
             {"expert": toward},
         )
 
     def near_wait(dst):
-        for kind in range(2):
-            near(kind, dst, dst, z_next).wait_recv()
+        near(dst, dst, z_next).wait_recv()
 
     def near_pass(src, dst, toward):
-        for kind in range(2):
-            near(kind, src, dst, toward).start()
+        near(src, dst, toward).start()
 
     def far_wait(dst):
-        for kind in range(2):
-            far(kind, dst, dst, z_next).wait_recv()
+        far(dst, dst, z_next).wait_recv()
 
     def far_pass(src, dst, toward):
-        for kind in range(2):
-            far(kind, src, dst, toward).start()
+        far(src, dst, toward).start()
 
     @pl.when(half == 0)
     def _():
@@ -289,12 +300,11 @@
             near_wait(4)
             near_pass(4, 6, z_next)
             near_wait(5)
-            near(0, 5, 7, z_last).start()
+            near_pass(5, 7, z_last)
 
         @pl.when(c == 3)
         def _():
             near_wait(6)
-            near(1, 6, 7, z_next).start()
             near_wait(7)
 
         @pl.when(c > 3)
@@ -317,26 +327,15 @@
     def take(c):
         pl.when(half == 0)(functools.partial(take_first, c))
         pl.when(half == 1)(functools.partial(take_second, c))
-        twin_x(c, half).start()
-        twin_d(c, half).start()
-
-    def twin_x(c, block):
+        twin(c, half).start()
+
+    def twin(c, block):
         span = pl.ds(c * SPAN, SPAN)
         return remote(
-            unit_x.at[block, span],
-            unit_x.at[block, span],
-            twin_sem.at[0, 0, c],
-            twin_sem.at[0, 1, c],
-            {"half": other},
-        )
-
-    def twin_d(c, block):
-        span = pl.ds(c * SPAN, SPAN)
-        return remote(
-            unit_d.at[block, span],
-            unit_d.at[block, span],
-            twin_sem.at[1, 0, c],
-            twin_sem.at[1, 1, c],
+            units.at[block, span],
+            units.at[block, span],
+            twin_sem.at[0, c],
+            twin_sem.at[1, c],
             {"half": other},
         )
 
@@ -370,13 +369,13 @@
 
     def select(c):
         chunk = order(c)
-        twin_x(chunk, other).wait_recv()
-        twin_d(chunk, other).wait_recv()
+        twin(chunk, other).wait_recv()
         span = pl.ds(chunk * SPAN, SPAN)
-        block_x = [unit_x[b, span].reshape(SPAN * UNIT_TOK, width + LANES) for b in range(2)]
-        all_x = jnp.concatenate(block_x, axis=0)
+        stacked = jnp.concatenate(
+            [units[b, span].reshape(SPAN * UNIT_TOK, 2 * width + LANES) for b in range(2)], axis=0
+        )
         is_expert = lax.broadcasted_iota(jnp.int32, (8, LANES), 1) == expert
-        gate_row = matmul(is_expert.astype(BF16), all_x[:, width:], 1, 1)
+        gate_row = matmul(is_expert.astype(BF16), stacked[:, width : width + LANES], 1, 1)
         chosen = gate_row > 0.0
         rank = matmul(chosen.astype(BF16), before_chunk[...])
         token = index_of((8, TOKENS), 1)
@@ -389,10 +388,9 @@
             pick, jnp.broadcast_to(gate_row[:1], (LANES, TOKENS)).astype(BF16), 1, 1
         )
         gates[c] = gate_wide
-        slots = matmul(pick, all_x[:, :width]).astype(BF16)
+        slots = matmul(pick, stacked[:, :width]).astype(BF16)
         slot_x[c] = slots
-        block_d = [unit_d[b, span].reshape(SPAN * UNIT_TOK, width) for b in range(2)]
-        slots_d = matmul(pick, jnp.concatenate(block_d, axis=0))
+        slots_d = matmul(pick, stacked[:, width + LANES :])
         slot_s[c] = (gate_wide[:, :1] * slots_d).astype(BF16)
         shape = (NY, PART, hidden)
         part[c, :, :, 0:hidden] = matmul(slots, w_gate[...]).astype(BF16).reshape(shape)
@@ -517,6 +515,38 @@
     for load in loads:
         load.wait()
 
+    def sent(c):
+        twin(c, half).wait_send()
+        for way in range(2):
+            first_sum(c, way).wait_send()
+            second_sum(c, way).wait_send()
+            act_copy(0, c, way, act.at[c, dp]).wait_send()
+            act_copy(1, c, way, act.at[c, y_far, :, columns(way)]).wait_send()
+        half_copy(c).wait_send()
+
+        @pl.when(c == 0)
+        def _():
+            for dst in range(1, NX):
+                near(0, dst, z_next).wait_send()
+
+        @pl.when((c == 0) & (half == 1))
+        def _():
+            for dst in range(NX, NZ):
+                near(0, dst, z_next).wait_send()
+
+        @pl.when((c > 3) | ((c > 1) & (half == 0)))
+        def _():
+            far(0, c, z_next).wait_send()
+
+        @pl.when(c == 2)
+        def _():
+            back_copy(1, 0, 0, z_next).wait_send()
+
+        @pl.when(c > 2)
+        def _():
+            for j in range(SPAN):
+                back_copy((c - 2) * SPAN + j, 0, 0, z_next).wait_send()
+
     def turn(i, carry):
         def staged(lag, work):
             pl.when((i >= lag) & (i - lag < CHUNKS))(functools.partial(work, i - lag))
@@ -536,9 +566,16 @@
         staged(9, row_terms)
         staged(10, give_back)
         staged(11, weight_terms)
+        staged(11, sent)
         return carry
 
     lax.fori_loop(0, CHUNKS + 11, turn, 0)
+
+    stores = []
+    for n in range(3):
+        grads_out[n] = acc[:, n * hidden : (n + 1) * hidden].astype(BF16)
+        stores.append(pltpu.make_async_copy(grads_out.at[n], grads_hbm.at[n], load_sem.at[3 + n]))
+        stores[n].start()
 
     own_gate = own_rows[:, width : width + LANES]
     own_chosen = (own_gate.astype(F32) > 0.0).astype(BF16)
@@ -594,115 +631,63 @@
     for r in range(1, NY):
         fin_copy(r).start()
     fin_recv[dp] = fin_send[dp]
-    for n in range(3):
-        grads_out[n] = acc[:, n * hidden : (n + 1) * hidden].astype(BF16)
-    store = pltpu.make_async_copy(grads_out, grads_hbm, load_sem.at[3])
-    store.start()
     for r in range(1, NY):
         fin_arrival(r).wait_recv()
     routes = jnp.zeros((PAD, LANES), F32)
     for q in range(NY):
         token_out[:, q * width : (q + 1) * width] = fin_recv[q, :, 0:width]
         routes = routes + fin_recv[q, :, width:].astype(F32)
-    lane = lax.broadcasted_iota(jnp.int32, (PAD, LANES), 1)
-    named = jnp.zeros((PAD, LANES), F32)
-    for k in range(8):
-        value = jnp.sum(jnp.where(ids[:, k : k + 1] == lane, routes, 0.0), axis=1, keepdims=True)
-        named = jnp.where(lane == k, value, named)
-    route_out[...] = named
-
-    store.wait()
+    unit = jnp.where(index_of((LANES, LANES), 0) == index_of((LANES, LANES), 1), 1.0, 0.0)
+    by_expert = matmul(unit.astype(BF16), routes.astype(BF16), 1, 1)[:, :TOK]
+    lane = lax.broadcasted_iota(jnp.int32, (LANES, TOK), 0)
+    named = ids[half]
+    for k in range(TOP):
+        value = jnp.where(named[k : k + 1] == lane, by_expert, 0.0)
+        route_out[k : k + 1] = jnp.sum(value, axis=0, keepdims=True)
+    for store in stores:
+        store.wait()
     for r in range(1, NY):
         own_copy(r).wait_send()
         fin_copy(r).wait_send()
 
-    for kind in range(2):
-        for dst in range(1, NX):
-            near(kind, 0, dst, z_next).wait_send()
-
-        @pl.when(half == 0)
-        def _(kind=kind):
-            far(kind, 0, 2, z_next).wait_send()
-            far(kind, 0, 3, z_next).wait_send()
-
-        @pl.when(half == 1)
-        def _(kind=kind):
-            for dst in range(NX, NZ):
-                near(kind, 0, dst, z_next).wait_send()
-
-        for dst in range(4, CHUNKS):
-            far(kind, 0, dst, z_next).wait_send()
-
-    def chunk_left(c, carry):
-        twin_x(c, half).wait_send()
-        twin_d(c, half).wait_send()
-        for way in range(2):
-            first_sum(c, way).wait_send()
-            second_sum(c, way).wait_send()
-            act_copy(0, c, way, act.at[c, dp]).wait_send()
-            act_copy(1, c, way, act.at[c, y_far, :, columns(way)]).wait_send()
-        half_copy(c).wait_send()
-        return carry
-
-    lax.fori_loop(0, CHUNKS, chunk_left, 0)
-
-    def back_left(place, carry):
+    for place in range((CHUNKS - 2) * SPAN, RING):
         back_copy(place, 0, 0, z_next).wait_send()
-        return carry
-
-    lax.fori_loop(1, RING, back_left, 0)
-
-
-def finish(token_rows, route_rows, grads, token_out, route_out, gate_out, up_out, down_out, sem):
-    copies = [
-        pltpu.make_async_copy(grads.at[n], target.at[0], sem.at[n])
-        for n, target in enumerate((gate_out, up_out, down_out))
-    ]
-    for copy in copies:
-        copy.start()
+
+
+def finish(token_rows, route_rows, grads, token_out, route_out, gate_out, up_out, down_out, held, sem):
+    targets = (gate_out, up_out, down_out)
+    loads = [pltpu.make_async_copy(grads.at[n], held.at[n], sem.at[0, n]) for n in range(3)]
+    stores = [pltpu.make_async_copy(held.at[n], targets[n].at[0], sem.at[1, n]) for n in range(3)]
+    for load in loads:
+        load.start()
     token_out[0, 0] = token_rows[:TOK]
-    route_out[0, 0] = route_rows[:TOK, : route_out.shape[3]].astype(BF16)
-    for copy in copies:
-        copy.wait()
+    route_out[0, 0] = route_rows[...].astype(BF16)
+    for load, store in zip(loads, stores):
+        load.wait()
+        store.start()
+    for store in stores:
+        store.wait()
 
 
 def on_device(tokens_in, cotangent, expert_ids, gate_probs, gate_weight, up_weight, down_weight):
-    half = lax.axis_index("half")
     width, hidden = gate_weight.shape[1], gate_weight.shape[2]
-
-    def block(values):
-        return jnp.where(half == 0, values[0, 0], values[0, 1])
-
-    def slices(values):
-        return block(values).reshape(TOK, NY, width).transpose(1, 0, 2)
-
-    ids = block(expert_ids)
-    named = ids[:, :, None] == jnp.arange(LANES, dtype=jnp.int32)
-    gate_map = jnp.sum(jnp.where(named, block(gate_probs).astype(F32)[:, :, None], 0.0), axis=1)
-    gate_map = jnp.broadcast_to(gate_map.astype(BF16)[None], (NY, TOK, LANES))
-    stage = jnp.concatenate([slices(tokens_in), gate_map, slices(cotangent)], axis=2)
-    stage = jnp.pad(stage, ((0, 0), (0, PAD - TOK), (0, 0)))
-    ids = jnp.pad(ids, ((0, PAD - TOK), (0, LANES - ids.shape[1])), constant_values=-1)
-
+    three = 3 * hidden
     vmem = pl.BlockSpec(memory_space=pltpu.VMEM)
     hbm = pl.BlockSpec(memory_space=pl.ANY)
-    three = 3 * hidden
-    weights = jax.ShapeDtypeStruct((1, width, hidden), BF16)
     out = pl.pallas_call(
         functools.partial(kernel, width, hidden),
         out_shape=(
             jax.ShapeDtypeStruct((PAD, NY * width), BF16),
-            jax.ShapeDtypeStruct((PAD, LANES), F32),
+            jax.ShapeDtypeStruct((TOP, TOK), F32),
             jax.ShapeDtypeStruct((3, width, hidden), BF16),
         ),
-        in_specs=[vmem] + [hbm] * 3 + [vmem],
+        in_specs=[vmem] * 4 + [hbm] * 3,
         out_specs=(vmem, vmem, hbm),
         scratch_shapes=[
             *[pltpu.VMEM((width, hidden), BF16)] * 3,
             pltpu.VMEM((TOKENS, TOKENS), BF16),
-            pltpu.VMEM((NY, PAD, 2 * width + LANES), BF16),
-            pltpu.VMEM((2, RING, UNIT_TOK, width + LANES), BF16),
-            pltpu.VMEM((2, RING, UNIT_TOK, width), BF16),
+            *[pltpu.VMEM((NY, PAD, 2 * width + LANES), BF16)] * 2,
+            pltpu.VMEM((2, RING, UNIT_TOK, 2 * width + LANES), BF16),
             pltpu.VMEM((CHUNKS, SLOTS, width), BF16),
             pltpu.VMEM((CHUNKS, SLOTS, width), BF16),
             pltpu.VMEM((CHUNKS, SLOTS, LANES), F32),
@@ -719,34 +704,44 @@
             pltpu.VMEM((width, three), F32),
             pltpu.VMEM((3, width, hidden), BF16),
             pltpu.SemaphoreType.DMA((2, NY)),
-            pltpu.SemaphoreType.DMA((2, 2, NZ)),
-            pltpu.SemaphoreType.DMA((2, 2, CHUNKS)),
-            pltpu.SemaphoreType.DMA((2, 2, CHUNKS)),
+            pltpu.SemaphoreType.DMA((2, NZ)),
+            pltpu.SemaphoreType.DMA((2, CHUNKS)),
+            pltpu.SemaphoreType.DMA((2, CHUNKS)),
             pltpu.SemaphoreType.DMA((2, 2, 2, CHUNKS)),
             pltpu.SemaphoreType.DMA((2, 2, 2, CHUNKS)),
             pltpu.SemaphoreType.DMA((2, CHUNKS)),
             pltpu.SemaphoreType.DMA((RING,)),
             pltpu.SemaphoreType.DMA((RING,)),
             pltpu.SemaphoreType.DMA((2, NY)),
-            pltpu.SemaphoreType.DMA((4,)),
+            pltpu.SemaphoreType.DMA((6,)),
         ],
         compiler_params=pltpu.CompilerParams(
             collective_id=0, has_side_effects=True, vmem_limit_bytes=62 * 1024 * 1024
         ),
-    )(stage, gate_weight[0], up_weight[0], down_weight[0], ids)
-    return pl.pallas_call(
+    )(
+        tokens_in[0].transpose(1, 0, 2),
+        cotangent[0].transpose(1, 0, 2),
+        expert_ids[0].transpose(0, 2, 1),
+        gate_probs[0].transpose(0, 2, 1),
+        gate_weight[0],
+        up_weight[0],
+        down_weight[0],
+    )
+    weights = jax.ShapeDtypeStruct((1, width, hidden), BF16)
+    token_grad, route_grad, *grads = pl.pallas_call(
         finish,
         out_shape=(
             jax.ShapeDtypeStruct((1, 1, TOK, NY * width), BF16),
-            jax.ShapeDtypeStruct((1, 1, TOK, expert_ids.shape[3]), BF16),
+            jax.ShapeDtypeStruct((1, 1, TOP, TOK), BF16),
             weights,
             weights,
             weights,
         ),
         in_specs=[vmem, vmem, hbm],
         out_specs=(vmem, vmem, hbm, hbm, hbm),
-        scratch_shapes=[pltpu.SemaphoreType.DMA((3,))],
+        scratch_shapes=[pltpu.VMEM((3, width, hidden), BF16), pltpu.SemaphoreType.DMA((2, 3))],
     )(*out)
+    return token_grad, route_grad.transpose(0, 1, 3, 2), *grads
 
 
 def solution(mesh):

time: 235 us -> 142 us (0.60)
  Pallas kernels: 225 us -> 140 us
  other arithmetic: 4.46 us -> 0 us
    pallas_call x1, Pallas kernels: 86.1 us -> 4.31 us  [on_device(): pl.pallas_call(finish, out_shape=(jax.ShapeDtypeStruct((1, 1, TOK, NY * w...]
    pallas_call x1, Pallas kernels: 139 us -> 136 us  [on_device(): pl.pallas_call(functools.partial(kernel, width, hidden), out_shape=(jax.S...]
    select_n x2 -> x0, other arithmetic: 2.91 us -> none  [block(): return jnp.where(half == 0, values[0, 0], values[0, 1])]
where the time goes in v3:
time: 142 us; the launch traced here: 140 us
  Pallas kernels  140 us (99%)
    pallas_call x1, Pallas kernels, on_device(): pl.pallas_call(functools.partial(kernel, width, hidden), out_shape=(jax.S...  136 us
    pallas_call x1, Pallas kernels, on_device(): pl.pallas_call(finish, out_shape=(jax.ShapeDtypeStruct((1, 1, TOK, NY * w...  4.31 us

profile of v3, /device:TPU:6, one launch (start us, length us, event | category | flops | bytes accessed | tf_op | source)
XLA Modules:
  0.0 140.5 jit_solution(9209079352281882694)
XLA Ops:
  0.6 135.5 %shard_map.110 = (bf16[16,3584]{1,0:T(8,128)(2,1)}, f32[8,12]{1,0:T(8,128)}, bf16[3,896,512]{2,1,0:T(8,128)(2,1)}) custom-call(bf16[12,2,3584]{2,1,0:T(2,128)(2,1)} %bitcast.19, bf16[12,2,3584]{2,1,0:T(2,128)(2,1)} %bitcast.20, s32[2,8,12]{2,1,0:T(8,128)} %bitcast.21, bf16[2,8,12]{2,1,0:T(8,128)(2,1)} %bitcast.22, bf16[896,512]{1,0:T(8,128)(2,1)} %bitcast.16, ...), custom_call_target="tpu_custom_call" | custom-call | tf_op jit(solution)/shard_map/pallas_call | solution.py:677
  136.2 4.3 %shard_map.111 = (bf16[1,1,12,3584]{3,2,1,0:T(8,128)(2,1)}, bf16[1,1,8,12]{3,2,1,0:T(8,128)(2,1)}, bf16[1,896,512]{2,1,0:T(8,128)(2,1)}, bf16[1,896,512]{2,1,0:T(8,128)(2,1)}, bf16[1,896,512]{2,1,0:T(8,128)(2,1)}) custom-call(bf16[16,3584]{1,0:T(8,128)(2,1)} %get-tuple-element.13.token_rows, f32[8,12]{1,0:T(8,128)} %get-tuple-element.14.route_rows, ...), custom_call_target="tpu_custom_call" | custom-call | tf_op jit(solution)/shard_map/pallas_call | solution.py:731

commit v4 on v3

--- a/solution.py
+++ b/solution.py
@@ -554,6 +554,7 @@
         staged(7, pass_act)
         staged(5, activate)
         staged(3, add_passing)
+        staged(8, row_terms)
         staged(1, select)
         first = i + jnp.where(i > 4, 1, 0)
         beyond = jnp.minimum(i + 1 + jnp.where(i > 3, 1, 0), CHUNKS)
@@ -563,13 +564,12 @@
             return carry
 
         lax.fori_loop(first, beyond, take_one, 0)
-        staged(9, row_terms)
-        staged(10, give_back)
-        staged(11, weight_terms)
-        staged(11, sent)
+        staged(8, give_back)
+        staged(9, weight_terms)
+        staged(10, sent)
         return carry
 
-    lax.fori_loop(0, CHUNKS + 11, turn, 0)
+    lax.fori_loop(0, CHUNKS + 10, turn, 0)
 
     stores = []
     for n in range(3):

time: 142 us -> 139 us (0.979)
  Pallas kernels: 140 us -> 138 us
    pallas_call x1, Pallas kernels: 136 us -> 134 us  [on_device(): pl.pallas_call(functools.partial(kernel, width, hidden), out_shape=(jax.S...]
where the time goes in v4:
time: 139 us
  Pallas kernels  138 us (99%)
    pallas_call x1, Pallas kernels, on_device(): pl.pallas_call(functools.partial(kernel, width, hidden), out_shape=(jax.S...  134 us
    pallas_call x1, Pallas kernels, on_device(): pl.pallas_call(finish, out_shape=(jax.ShapeDtypeStruct((1, 1, TOK, NY * w...  4.31 us

profile of v4, /device:TPU:6, one launch (start us, length us, event | category | flops | bytes accessed | tf_op | source)
XLA Modules:
  0.0 138.8 jit_solution(5281849571677327970)
XLA Ops:
  0.6 133.8 %shard_map.110 = (bf16[16,3584]{1,0:T(8,128)(2,1)}, f32[8,12]{1,0:T(8,128)}, bf16[3,896,512]{2,1,0:T(8,128)(2,1)}) custom-call(bf16[12,2,3584]{2,1,0:T(2,128)(2,1)} %bitcast.19, bf16[12,2,3584]{2,1,0:T(2,128)(2,1)} %bitcast.20, s32[2,8,12]{2,1,0:T(8,128)} %bitcast.21, bf16[2,8,12]{2,1,0:T(8,128)(2,1)} %bitcast.22, bf16[896,512]{1,0:T(8,128)(2,1)} %bitcast.16, ...), custom_call_target="tpu_custom_call" | custom-call | tf_op jit(solution)/shard_map/pallas_call | solution.py:677
  134.5 4.3 %shard_map.111 = (bf16[1,1,12,3584]{3,2,1,0:T(8,128)(2,1)}, bf16[1,1,8,12]{3,2,1,0:T(8,128)(2,1)}, bf16[1,896,512]{2,1,0:T(8,128)(2,1)}, bf16[1,896,512]{2,1,0:T(8,128)(2,1)}, bf16[1,896,512]{2,1,0:T(8,128)(2,1)}) custom-call(bf16[16,3584]{1,0:T(8,128)(2,1)} %get-tuple-element.13.token_rows, f32[8,12]{1,0:T(8,128)} %get-tuple-element.14.route_rows, ...), custom_call_target="tpu_custom_call" | custom-call | tf_op jit(solution)/shard_map/pallas_call | solution.py:731

commit v5 on v4

--- a/solution.py
+++ b/solution.py
@@ -551,11 +551,11 @@
         def staged(lag, work):
             pl.when((i >= lag) & (i - lag < CHUNKS))(functools.partial(work, i - lag))
 
-        staged(7, pass_act)
-        staged(5, activate)
+        staged(6, pass_act)
         staged(3, add_passing)
-        staged(8, row_terms)
+        staged(7, row_terms)
         staged(1, select)
+        staged(4, activate)
         first = i + jnp.where(i > 4, 1, 0)
         beyond = jnp.minimum(i + 1 + jnp.where(i > 3, 1, 0), CHUNKS)
 
@@ -564,12 +564,12 @@
             return carry
 
         lax.fori_loop(first, beyond, take_one, 0)
-        staged(8, give_back)
-        staged(9, weight_terms)
-        staged(10, sent)
+        staged(7, give_back)
+        staged(8, weight_terms)
+        staged(9, sent)
         return carry
 
-    lax.fori_loop(0, CHUNKS + 10, turn, 0)
+    lax.fori_loop(0, CHUNKS + 9, turn, 0)
 
     stores = []
     for n in range(3):

time: 139 us -> 138 us (level)
  no operation moved by 1% of the time
where the time goes in v5:
time: 138 us
  Pallas kernels  137 us (99%)
    pallas_call x1, Pallas kernels, on_device(): pl.pallas_call(functools.partial(kernel, width, hidden), out_shape=(jax.S...  133 us
    pallas_call x1, Pallas kernels, on_device(): pl.pallas_call(finish, out_shape=(jax.ShapeDtypeStruct((1, 1, TOK, NY * w...  4.31 us

profile of v5, /device:TPU:6, one launch (start us, length us, event | category | flops | bytes accessed | tf_op | source)
XLA Modules:
  0.0 137.7 jit_solution(2656844240118818159)
XLA Ops:
  0.6 132.8 %shard_map.110 = (bf16[16,3584]{1,0:T(8,128)(2,1)}, f32[8,12]{1,0:T(8,128)}, bf16[3,896,512]{2,1,0:T(8,128)(2,1)}) custom-call(bf16[12,2,3584]{2,1,0:T(2,128)(2,1)} %bitcast.19, bf16[12,2,3584]{2,1,0:T(2,128)(2,1)} %bitcast.20, s32[2,8,12]{2,1,0:T(8,128)} %bitcast.21, bf16[2,8,12]{2,1,0:T(8,128)(2,1)} %bitcast.22, bf16[896,512]{1,0:T(8,128)(2,1)} %bitcast.16, ...), custom_call_target="tpu_custom_call" | custom-call | tf_op jit(solution)/shard_map/pallas_call | solution.py:677
  133.4 4.3 %shard_map.111 = (bf16[1,1,12,3584]{3,2,1,0:T(8,128)(2,1)}, bf16[1,1,8,12]{3,2,1,0:T(8,128)(2,1)}, bf16[1,896,512]{2,1,0:T(8,128)(2,1)}, bf16[1,896,512]{2,1,0:T(8,128)(2,1)}, bf16[1,896,512]{2,1,0:T(8,128)(2,1)}) custom-call(bf16[16,3584]{1,0:T(8,128)(2,1)} %get-tuple-element.13.token_rows, f32[8,12]{1,0:T(8,128)} %get-tuple-element.14.route_rows, ...), custom_call_target="tpu_custom_call" | custom-call | tf_op jit(solution)/shard_map/pallas_call | solution.py:731
